TPU v7x, 32 devices: a whole 2x2x4 slice. The times are simulated.
32 devices in a mesh: gx: 4 (over y, x), gy: 4 (over z), gz: 2 (over core).
Axes of the slice: x: 2, y: 2, z: 4, core: 2. Of those that a mesh axis runs over, the one named last changes fastest.
Arguments:
- offsets: float32 [3, 16, 16, 8, 128], P(None, 'gx', 'gy', 'gz'), may hold values from 0 to 1
- masses: float32 [16, 16, 8, 128], P('gx', 'gy', 'gz'), may hold values from 2e-05 to 0.0002
- counts: int32 [16, 16, 8], P('gx', 'gy', 'gz'), may hold values from 1 to 128, as said below
Outputs:
- potential: float32 [16, 16, 8, 128], P('gx', 'gy', 'gz')
- near_part: float32 [16, 16, 8, 128], P('gx', 'gy', 'gz')
- far_leaf: float32 [16, 16, 8, 128], P('gx', 'gy', 'gz')
Inputs may be any that keep to these rules, and one draw needn't show every extreme that they name: counts gives the live slots of each leaf; slots from counts on have masses that do not enter; some leaf holds 128 particles.
All inputs are finite; a program needn't handle non-finite values.
Results may differ from a plain program's by a relative error of at most 0.0003.
Values sent between devices are 32-bit elements; how exact they have to be, the bound alone decides.
A program may use at most 320 MiB of HBM per device.

v0:
```python
import math

import jax
import jax.numpy as jnp
from jax import lax
from jax.sharding import PartitionSpec as P

ORDER = 8


HIGHEST = lax.Precision.HIGHEST
SOFTENING = 0.02


def with_halo(shard, sides, width):
    for axis, dim in sides:
        peers, length = (lax.axis_size(axis), shard.shape[dim])
        up = [(i, (i + 1) % peers) for i in range(peers - 1)]
        down = [(j, i) for i, j in up]
        last = lax.slice_in_dim(shard, length - width, length, axis=dim)
        leading = lax.slice_in_dim(shard, 0, width, axis=dim)
        before = lax.ppermute(last, axis, up)
        after = lax.ppermute(leading, axis, down)
        shard = jnp.concatenate([before, shard, after], axis=dim)
    return shard


def expansion_tables(top_order):
    powers_list = []
    for degree in range(top_order + 1):
        for first_part in range(degree, -1, -1):
            for second_part in range(degree - first_part, -1, -1):
                powers_list.append((first_part, second_part, degree - first_part - second_part))
    position = {entry: number for number, entry in enumerate(powers_list)}
    return (powers_list, position)


def translation_tables(top_order):
    powers_list, position = expansion_tables(top_order)
    n_terms = len(powers_list)
    source_index = [[0] * n_terms for unused in range(n_terms)]
    weights = [[0.0] * n_terms for unused in range(n_terms)]
    for j_entry, j_power in enumerate(powers_list):
        for k_entry, k_power in enumerate(powers_list):
            joined = tuple((j_power[d] + k_power[d] for d in range(3)))
            if sum(joined) <= top_order:
                source_index[j_entry][k_entry] = position[joined]
                factor = (-1.0) ** sum(k_power)
                for d in range(3):
                    factor = factor * math.comb(joined[d], j_power[d])
                weights[j_entry][k_entry] = factor
    return (jnp.asarray(source_index, jnp.int32), jnp.asarray(weights, jnp.float32))


def shift_matrices(top_order, child_size):
    powers_list, position = expansion_tables(top_order)
    n_terms = len(powers_list)
    result = [[[0.0] * n_terms for unused in range(n_terms)] for other in range(8)]
    for child in range(8):
        bits = (child >> 2 & 1, child >> 1 & 1, child & 1)
        offset = [(bits[d] - 0.5) * child_size for d in range(3)]
        for k_entry, k_power in enumerate(powers_list):
            for i_entry, i_power in enumerate(powers_list):
                if all((i_power[d] <= k_power[d] for d in range(3))):
                    factor = 1.0
                    for d in range(3):
                        factor = (
                            factor
                            * math.comb(k_power[d], i_power[d])
                            * offset[d] ** (k_power[d] - i_power[d])
                        )
                    result[child][k_entry][i_entry] = factor
    return jnp.asarray(result, jnp.float32)


def taylor_terms(vector, top_order):
    powers_list, position = expansion_tables(top_order)
    radius_sq = vector[0] * vector[0] + vector[1] * vector[1] + vector[2] * vector[2]
    taylor_rows = [1.0 / jnp.sqrt(radius_sq)]
    for entry in range(1, len(powers_list)):
        exponent = powers_list[entry]
        degree = sum(exponent)
        linear_part = jnp.zeros_like(radius_sq)
        square_part = jnp.zeros_like(radius_sq)
        for axis_id in range(3):
            if exponent[axis_id] >= 1:
                lowered = list(exponent)
                lowered[axis_id] -= 1
                linear_part = linear_part + vector[axis_id] * taylor_rows[position[tuple(lowered)]]
            if exponent[axis_id] >= 2:
                lowered = list(exponent)
                lowered[axis_id] -= 2
                square_part = square_part + taylor_rows[position[tuple(lowered)]]
        taylor_rows.append(
            -((2 * degree - 1) * linear_part + (degree - 1) * square_part) / (degree * radius_sq)
        )
    return jnp.stack(taylor_rows)


def monomials(positions, top_order):
    powers_list, position = expansion_tables(top_order)
    centred = positions - 0.5
    picked = []
    for d in range(3):
        ladder = [jnp.ones_like(centred[d])]
        for step in range(top_order):
            ladder.append(ladder[-1] * centred[d])
        select = [
            [1.0 if entry[d] == level else 0.0 for level in range(top_order + 1)]
            for entry in powers_list
        ]
        picked.append(
            jnp.tensordot(
                jnp.asarray(select, jnp.float32), jnp.stack(ladder), axes=1, precision=HIGHEST
            )
        )
    return picked[0] * picked[1] * picked[2]


def near_field(window):
    a, b, c = (window.shape[1] - 2, window.shape[2] - 2, window.shape[3] - 2)
    centre = window[:, 1:-1, 1:-1, 1:-1]
    total = jnp.zeros(centre.shape[1:], jnp.float32)
    for p in range(3):
        for q in range(3):
            for r in range(3):
                source = window[:, p : p + a, q : q + b, r : r + c]
                squared = SOFTENING * SOFTENING
                for axis_id, shift in enumerate((p - 1, q - 1, r - 1)):
                    gap = (
                        source[axis_id][..., None, :] + float(shift) - centre[axis_id][..., :, None]
                    )
                    squared = squared + gap * gap
                total = total + jnp.sum(source[3][..., None, :] / jnp.sqrt(squared), axis=-1)
    return total - centre[3] / SOFTENING


def window_kernel(step, top_order):
    source_index, weights = translation_tables(top_order)
    grid = jnp.arange(7, dtype=jnp.float32) - 3.0
    mesh = jnp.meshgrid(grid, grid, grid, indexing="ij")
    vx, vy, vz = [m.reshape(-1) for m in mesh]
    near = (jnp.abs(vx) <= 1.0) & (jnp.abs(vy) <= 1.0) & (jnp.abs(vz) <= 1.0)
    vector = jnp.stack(
        [
            jnp.where(near, 4.0, -vx) * step,
            jnp.where(near, 0.0, -vy) * step,
            jnp.where(near, 0.0, -vz) * step,
        ]
    )
    terms = taylor_terms(vector, top_order)
    kernel = terms[source_index] * weights[:, :, None]
    return jnp.transpose(kernel, (2, 0, 1))


def interaction_mask(extents, anchor):
    offsets_list = jnp.arange(7, dtype=jnp.int32) - 3
    valid = []
    for d in range(3):
        cells = jnp.arange(extents[d], dtype=jnp.int32) + anchor[d]
        moved = (
            jnp.floor_divide(cells[None, :] + offsets_list[:, None], 2)
            - jnp.floor_divide(cells, 2)[None, :]
        )
        valid.append(jnp.abs(moved) <= 1)
    far = jnp.abs(offsets_list) >= 2
    separated = far[:, None, None] | far[None, :, None] | far[None, None, :]
    mask = (
        valid[0][:, None, None, :, None, None]
        & valid[1][None, :, None, None, :, None]
        & valid[2][None, None, :, None, None, :]
    )
    mask = mask & separated[:, :, :, None, None, None]
    return mask.reshape(343, extents[0] * extents[1] * extents[2]).astype(jnp.float32)


def window_interactions(window, kernel, anchor):
    a, b, c, n_terms = (
        window.shape[0] - 6,
        window.shape[1] - 6,
        window.shape[2] - 6,
        window.shape[3],
    )
    along_x = jnp.stack([window[s : s + a] for s in range(7)])
    along_y = jnp.stack([along_x[:, :, s : s + b] for s in range(7)], axis=1)
    along_z = jnp.stack([along_y[:, :, :, :, s : s + c] for s in range(7)], axis=2)
    gathered = (
        along_z.reshape(343, a * b * c, n_terms) * interaction_mask((a, b, c), anchor)[:, :, None]
    )
    result = jnp.einsum("vcm,vjm->cj", gathered, kernel, precision=HIGHEST)
    return result.reshape(a, b, c, n_terms)


def cell_centers(starts, extents, size):
    grids = jnp.meshgrid(
        *[jnp.arange(extents[d], dtype=jnp.int32) + starts[d] for d in range(3)], indexing="ij"
    )
    return jnp.stack([g.reshape(-1).astype(jnp.float32) * size + 0.5 * size for g in grids], axis=1)


def pair_interactions(target_centers, source_moments, source_centers, step, top_order):
    source_index, weight_table = translation_tables(top_order)

    def one_target(center):

        def add_block(total, pieces):
            moments, centers = pieces
            gap = center[None, :] - centers
            near = jnp.max(jnp.abs(gap), axis=1) <= 1.5 * step
            vector = jnp.stack(
                [
                    jnp.where(near, 4.0 * step, gap[:, 0]),
                    jnp.where(near, 0.0, gap[:, 1]),
                    jnp.where(near, 0.0, gap[:, 2]),
                ]
            )
            terms = taylor_terms(vector, top_order)
            kernel = terms[source_index] * weight_table[:, :, None]
            kept = moments * jnp.where(near, 0.0, 1.0)[:, None]
            return (total + jnp.einsum("jkb,bk->j", kernel, kept, precision=HIGHEST), None)

        start = jnp.zeros((source_moments.shape[-1],), jnp.float32)
        total, unused = lax.scan(add_block, start, (source_moments, source_centers))
        return total

    return lax.map(one_target, target_centers)


def up_shift(moments, matrices):
    a, b, c, n_terms = moments.shape
    grouped = moments.reshape(a // 2, 2, b // 2, 2, c // 2, 2, n_terms).transpose(
        0, 2, 4, 1, 3, 5, 6
    )
    grouped = grouped.reshape(a // 2, b // 2, c // 2, 8, n_terms)
    return jnp.einsum("xyzgi,gki->xyzk", grouped, matrices, precision=HIGHEST)


def down_shift(local, matrices):
    a, b, c, n_terms = local.shape
    spread = jnp.einsum("xyzk,gki->xyzgi", local, matrices, precision=HIGHEST)
    spread = spread.reshape(a, b, c, 2, 2, 2, n_terms).transpose(0, 3, 1, 4, 2, 5, 6)
    return spread.reshape(2 * a, 2 * b, 2 * c, n_terms)


def arrange_grid(gathered, span_x, span_y, span_z):
    a, b, c, n_terms = gathered.shape[1:]
    whole = gathered.reshape(span_x, span_y, span_z, a, b, c, n_terms).transpose(
        0, 3, 1, 4, 2, 5, 6
    )
    return whole.reshape(span_x * a, span_y * b, span_z * c, n_terms)


def shards(offsets, masses, counts):
    leaf_x, leaf_y, leaf_z = counts.shape
    slots = masses.shape[-1]
    tiles = leaf_x * leaf_y * leaf_z
    live = (jnp.arange(slots, dtype=jnp.int32)[None, None, None, :] < counts[..., None]).astype(
        jnp.float32
    )
    charge = masses * live
    packed = jnp.concatenate([offsets, charge[None]], axis=0)
    padded = with_halo(packed, (("gx", 1), ("gy", 2), ("gz", 3)), 1)
    near = near_field(padded)
    monomial_rows = monomials(offsets.reshape(3, tiles, slots), ORDER)
    n_terms = monomial_rows.shape[0]
    moments0 = jnp.einsum(
        "kts,ts->tk", monomial_rows, charge.reshape(tiles, slots), precision=HIGHEST
    )
    moments0 = moments0.reshape(leaf_x, leaf_y, leaf_z, n_terms)
    window0 = with_halo(moments0, (("gx", 0), ("gy", 1), ("gz", 2)), 3)
    local0 = window_interactions(window0, window_kernel(1.0, ORDER), (0, 0, 0))
    shift_leaf = shift_matrices(ORDER, 1.0)
    shift_mid = shift_matrices(ORDER, 2.0)
    moments1 = up_shift(moments0, shift_leaf)
    mid_x, mid_y, mid_z = (leaf_x // 2, leaf_y // 2, leaf_z // 2)
    top_x, top_y, top_z = (leaf_x // 4, leaf_y // 4, leaf_z // 4)
    span_x, span_y, span_z = (lax.axis_size("gx"), lax.axis_size("gy"), lax.axis_size("gz"))
    place_x, place_y, place_z = (lax.axis_index("gx"), lax.axis_index("gy"), lax.axis_index("gz"))
    gathered = lax.all_gather(moments1[None], ("gx", "gy", "gz"), axis=0, tiled=True)
    whole = arrange_grid(gathered, span_x, span_y, span_z)
    padded1 = jnp.pad(whole, ((3, 3), (3, 3), (3, 3), (0, 0)))
    window1 = lax.dynamic_slice(
        padded1,
        (place_x * mid_x, place_y * mid_y, place_z * mid_z, 0),
        (mid_x + 6, mid_y + 6, mid_z + 6, n_terms),
    )
    top_moments = up_shift(whole, shift_mid)
    local1 = window_interactions(window1, window_kernel(2.0, ORDER), (0, 0, 0))
    top_shape = top_moments.shape[:3]
    source_centers = cell_centers((0, 0, 0), top_shape, 4.0).reshape(-1, top_shape[2], 3)
    sources = top_moments.reshape(-1, top_shape[2], n_terms)
    target_centers = cell_centers(
        (place_x * top_x, place_y * top_y, place_z * top_z), (top_x, top_y, top_z), 4.0
    )
    local2 = pair_interactions(target_centers, sources, source_centers, 4.0, ORDER).reshape(
        top_x, top_y, top_z, n_terms
    )
    total1 = local1 + down_shift(local2, shift_mid)
    total0 = local0 + down_shift(total1, shift_leaf)
    far = jnp.einsum("kts,tk->ts", monomial_rows, total0.reshape(tiles, n_terms), precision=HIGHEST)
    far = far.reshape(leaf_x, leaf_y, leaf_z, slots)
    far_local = jnp.einsum(
        "kts,tk->ts", monomial_rows, local0.reshape(tiles, n_terms), precision=HIGHEST
    )
    far_local = far_local.reshape(leaf_x, leaf_y, leaf_z, slots)
    return (-(near + far) * live, -near * live, -far_local * live)


def solution(mesh):
    placed = (P(None, "gx", "gy", "gz", None), P("gx", "gy", "gz", None), P("gx", "gy", "gz"))
    return jax.shard_map(
        shards,
        mesh=mesh,
        in_specs=placed,
        out_specs=(P("gx", "gy", "gz", None), P("gx", "gy", "gz", None), P("gx", "gy", "gz", None)),
        check_vma=False,
    )
```

profile of v0, /device:TPU:5, one launch (start us, length us, event | category | flops | bytes accessed | tf_op | source)
XLA Modules:
  0.0 1740.0 jit_solution(746327212387973634)
XLA Ops:
  2.0 5.2 fusion.55
  7.3 4.5 fusion.57
  11.9 5.4 multiply_multiply_fusion
  19.6 8.6 fusion.15
  39.3 3.4 collective-permute-start.1
  72.8 43.0 %all-gather = f32[64,2,2,165]{3,2,1,0:T(2,128)S(1)} all-gather(f32[2,2,2,165]{3,2,1,0:T(2,128)S(1)} %convolution_bitcast_fusion.1), channel_id=2, replica_groups=mesh['gx'=4,'gy'=4,'gz'=2] {'gx','gy','gz'}, dimensions={0}, use_global_device_ids=true | all-gather | bytes 174240 | tf_op jit(solution)/shard_map/all_gather | solution.py:279
  120.9 3.5 reshape.23911
  133.9 8.2 stack.170
  142.1 67.6 %gather_fusion.2 = f32[27225,343]{1,0:T(8,128)} fusion(f32[165,343]{1,0:T(8,128)S(1)} %stack.170, s32[27648]{0:T(1024)S(1)} %pad_clamp_fusion.1), kind=kCustom, calls=%fused_computation.2 | custom fusion | bytes 74814304 | tf_op jit(solution)/shard_map/gather | solution.py:152
  210.1 35.9 %reshape.23940 = f32[165,165,343]{2,1,0:T(8,128)} reshape(f32[27225,343]{1,0:T(8,128)} %gather_fusion.2) | data formatting | bytes 74705400 | tf_op jit(solution)/shard_map/gather | solution.py:152
  247.0 4.1 stack.145
  251.0 67.4 %gather_fusion.1 = f32[27225,343]{1,0:T(8,128)} fusion(f32[165,343]{1,0:T(8,128)S(1)} %stack.145, s32[27648]{0:T(1024)S(1)} %pad_clamp_fusion.1), kind=kCustom, calls=%fused_computation.1 | custom fusion | bytes 74814304 | tf_op jit(solution)/shard_map/gather | solution.py:152
  318.5 36.0 %reshape.23932 = f32[165,165,343]{2,1,0:T(8,128)} reshape(f32[27225,343]{1,0:T(8,128)} %gather_fusion.1) | data formatting | bytes 74705400 | tf_op jit(solution)/shard_map/gather | solution.py:152
  356.3 986.8 %while.19 = (s32[]{:T(128)}, f32[165]{0:T(256)S(1)}, f32[3]{0:T(128)S(1)}, f32[16,2,3]{2,1,0:T(2,128)S(1)}, f32[16,2,165]{2,0,1:T(8,128)S(1)}, /*index=5*/s32[]{...) while((s32[]{:T(128)}, f32[165]{0:T(256)S(1)}, f32[3]{0:T(128)S(1)}, ...), condition=%wide.region_29.30_spmd.clone.clone, body=%wide.region_27.29_spmd.sunk.clone.clone.sunk | while | flops 739591 | bytes 1978783 | solution.py:223
  358.3 50.8 %gather_fusion = f32[27225,2]{1,0:T(8,128)} fusion(f32[165,2]{1,0:T(8,128)S(1)} %stack.180, s32[27648]{0:T(1024)S(1)} %pad_clamp_fusion.3), kind=kCustom, calls=%fused_computation.clone.clone.1 | custom fusion | bytes 544500 | tf_op jit(solution)/shard_map/while/body/eval_jaxpr/while/body/eval_jaxpr/gather | solution.py:218
  409.1 8.0 copy.570
  419.9 50.8 %gather_fusion = f32[27225,2]{1,0:T(8,128)} fusion(f32[165,2]{1,0:T(8,128)S(1)} %stack.180, s32[27648]{0:T(1024)S(1)} %pad_clamp_fusion.3), kind=kCustom, calls=%fused_computation.clone.clone.1 | custom fusion | bytes 544500 | tf_op jit(solution)/shard_map/while/body/eval_jaxpr/while/body/eval_jaxpr/gather | solution.py:218
  470.7 8.0 copy.570
  481.6 50.8 %gather_fusion = f32[27225,2]{1,0:T(8,128)} fusion(f32[165,2]{1,0:T(8,128)S(1)} %stack.180, s32[27648]{0:T(1024)S(1)} %pad_clamp_fusion.3), kind=kCustom, calls=%fused_computation.clone.clone.1 | custom fusion | bytes 544500 | tf_op jit(solution)/shard_map/while/body/eval_jaxpr/while/body/eval_jaxpr/gather | solution.py:218
  532.4 8.0 copy.570
  543.3 50.8 %gather_fusion = f32[27225,2]{1,0:T(8,128)} fusion(f32[165,2]{1,0:T(8,128)S(1)} %stack.180, s32[27648]{0:T(1024)S(1)} %pad_clamp_fusion.3), kind=kCustom, calls=%fused_computation.clone.clone.1 | custom fusion | bytes 544500 | tf_op jit(solution)/shard_map/while/body/eval_jaxpr/while/body/eval_jaxpr/gather | solution.py:218
  594.1 8.0 copy.570
  605.0 50.8 %gather_fusion = f32[27225,2]{1,0:T(8,128)} fusion(f32[165,2]{1,0:T(8,128)S(1)} %stack.180, s32[27648]{0:T(1024)S(1)} %pad_clamp_fusion.3), kind=kCustom, calls=%fused_computation.clone.clone.1 | custom fusion | bytes 544500 | tf_op jit(solution)/shard_map/while/body/eval_jaxpr/while/body/eval_jaxpr/gather | solution.py:218
  655.8 8.0 copy.570
  666.7 50.8 %gather_fusion = f32[27225,2]{1,0:T(8,128)} fusion(f32[165,2]{1,0:T(8,128)S(1)} %stack.180, s32[27648]{0:T(1024)S(1)} %pad_clamp_fusion.3), kind=kCustom, calls=%fused_computation.clone.clone.1 | custom fusion | bytes 544500 | tf_op jit(solution)/shard_map/while/body/eval_jaxpr/while/body/eval_jaxpr/gather | solution.py:218
  717.4 8.0 copy.570
  728.3 50.8 %gather_fusion = f32[27225,2]{1,0:T(8,128)} fusion(f32[165,2]{1,0:T(8,128)S(1)} %stack.180, s32[27648]{0:T(1024)S(1)} %pad_clamp_fusion.3), kind=kCustom, calls=%fused_computation.clone.clone.1 | custom fusion | bytes 544500 | tf_op jit(solution)/shard_map/while/body/eval_jaxpr/while/body/eval_jaxpr/gather | solution.py:218
  779.1 8.0 copy.570
  790.0 50.8 %gather_fusion = f32[27225,2]{1,0:T(8,128)} fusion(f32[165,2]{1,0:T(8,128)S(1)} %stack.180, s32[27648]{0:T(1024)S(1)} %pad_clamp_fusion.3), kind=kCustom, calls=%fused_computation.clone.clone.1 | custom fusion | bytes 544500 | tf_op jit(solution)/shard_map/while/body/eval_jaxpr/while/body/eval_jaxpr/gather | solution.py:218
  840.8 8.0 copy.570
  851.7 50.8 %gather_fusion = f32[27225,2]{1,0:T(8,128)} fusion(f32[165,2]{1,0:T(8,128)S(1)} %stack.180, s32[27648]{0:T(1024)S(1)} %pad_clamp_fusion.3), kind=kCustom, calls=%fused_computation.clone.clone.1 | custom fusion | bytes 544500 | tf_op jit(solution)/shard_map/while/body/eval_jaxpr/while/body/eval_jaxpr/gather | solution.py:218
  902.5 8.0 copy.570
  913.4 50.8 %gather_fusion = f32[27225,2]{1,0:T(8,128)} fusion(f32[165,2]{1,0:T(8,128)S(1)} %stack.180, s32[27648]{0:T(1024)S(1)} %pad_clamp_fusion.3), kind=kCustom, calls=%fused_computation.clone.clone.1 | custom fusion | bytes 544500 | tf_op jit(solution)/shard_map/while/body/eval_jaxpr/while/body/eval_jaxpr/gather | solution.py:218
  964.1 8.0 copy.570
  975.0 50.8 %gather_fusion = f32[27225,2]{1,0:T(8,128)} fusion(f32[165,2]{1,0:T(8,128)S(1)} %stack.180, s32[27648]{0:T(1024)S(1)} %pad_clamp_fusion.3), kind=kCustom, calls=%fused_computation.clone.clone.1 | custom fusion | bytes 544500 | tf_op jit(solution)/shard_map/while/body/eval_jaxpr/while/body/eval_jaxpr/gather | solution.py:218
  1025.8 8.0 copy.570
  1036.7 50.8 %gather_fusion = f32[27225,2]{1,0:T(8,128)} fusion(f32[165,2]{1,0:T(8,128)S(1)} %stack.180, s32[27648]{0:T(1024)S(1)} %pad_clamp_fusion.3), kind=kCustom, calls=%fused_computation.clone.clone.1 | custom fusion | bytes 544500 | tf_op jit(solution)/shard_map/while/body/eval_jaxpr/while/body/eval_jaxpr/gather | solution.py:218
  1087.5 8.0 copy.570
  1098.4 50.8 %gather_fusion = f32[27225,2]{1,0:T(8,128)} fusion(f32[165,2]{1,0:T(8,128)S(1)} %stack.180, s32[27648]{0:T(1024)S(1)} %pad_clamp_fusion.3), kind=kCustom, calls=%fused_computation.clone.clone.1 | custom fusion | bytes 544500 | tf_op jit(solution)/shard_map/while/body/eval_jaxpr/while/body/eval_jaxpr/gather | solution.py:218
  1149.2 8.0 copy.570
  1160.1 50.8 %gather_fusion = f32[27225,2]{1,0:T(8,128)} fusion(f32[165,2]{1,0:T(8,128)S(1)} %stack.180, s32[27648]{0:T(1024)S(1)} %pad_clamp_fusion.3), kind=kCustom, calls=%fused_computation.clone.clone.1 | custom fusion | bytes 544500 | tf_op jit(solution)/shard_map/while/body/eval_jaxpr/while/body/eval_jaxpr/gather | solution.py:218
  1210.8 8.0 copy.570
  1221.7 50.8 %gather_fusion = f32[27225,2]{1,0:T(8,128)} fusion(f32[165,2]{1,0:T(8,128)S(1)} %stack.180, s32[27648]{0:T(1024)S(1)} %pad_clamp_fusion.3), kind=kCustom, calls=%fused_computation.clone.clone.1 | custom fusion | bytes 544500 | tf_op jit(solution)/shard_map/while/body/eval_jaxpr/while/body/eval_jaxpr/gather | solution.py:218
  1272.5 8.0 copy.570
  1283.4 50.8 %gather_fusion = f32[27225,2]{1,0:T(8,128)} fusion(f32[165,2]{1,0:T(8,128)S(1)} %stack.180, s32[27648]{0:T(1024)S(1)} %pad_clamp_fusion.3), kind=kCustom, calls=%fused_computation.clone.clone.1 | custom fusion | bytes 544500 | tf_op jit(solution)/shard_map/while/body/eval_jaxpr/while/body/eval_jaxpr/gather | solution.py:218
  1334.2 8.0 copy.570
  1343.2 57.8 %multiply_bitcast_fusion.1 = (f32[343,165,165]{0,2,1:T(8,128)}, f32[343,165,165,1,1]{0,2,1,4,3:T(8,128)}) fusion(f32[165,165,343]{2,1,0:T(8,128)} %reshape.23932, f32[165,165]{1,0:T(8,128)S(1)} %get-tuple-element.1319, f32[165,165,343]{2,1,0:T(8,128)} %reshape.23940), kind=kLoop, calls=%fused_computation.208 | loop fusion | flops 18676350 | bytes 149519696 | tf_op jit(solution)/shard_map/mul | solution.py:152
  1402.2 52.5 %fusion.42 = f32[2,2,2,165,1]{3,2,4,1,0:T(2,128)S(1)} fusion(f32[343,165,165,1,1]{0,2,1,4,3:T(8,128)} %get-tuple-element.799, f32[2,2,2,165,343]{4,3,2,1,0:T(8,128)S(1)} %bitcast.512, f32[1,2,2,2,165]{4,0,3,2,1:T(1,128)S(1)} %fusion.165), kind=kOutput, calls=%fused_computation.286 | convolution fusion | flops 896466048 | bytes 39174300 | tf_op jit(solution)/shard_map/vcm,vjm->cj/dot_general | solution.py:190
  1462.6 4.0 collective-permute-start.2
  1473.7 3.8 collective-permute-start.5
  1484.8 12.5 multiply_reduce_fusion.13
  1497.3 9.2 multiply_reduce_fusion.2
  1506.5 12.5 multiply_reduce_fusion.14
  1519.1 12.5 multiply_reduce_fusion.26
  1531.6 12.5 multiply_reduce_fusion.18
  1544.2 12.5 multiply_reduce_fusion.6
  1556.8 12.8 multiply_reduce_fusion.25
  1591.3 15.6 copy.485
  1606.9 26.4 %reshape.23907 = f32[343,64,165]{2,1,0:T(8,128)} reshape(f32[7,7,7,4,4,4,165]{6,5,4,3,2,1,0:T(4,128)} %copy.485) | data formatting | bytes 28976640 | tf_op jit(solution)/shard_map/reshape | solution.py:188
  1633.3 17.8 %broadcast_multiply_fusion.14 = f32[343,64,165]{2,1,0:T(8,128)} fusion(f32[343,64,165]{2,1,0:T(8,128)} %reshape.23907, f32[343,64]{1,0:T(8,128)S(1)} %copy.486), kind=kLoop, calls=%fused_computation.209 | loop fusion | flops 3622080 | bytes 29064448 | tf_op jit(solution)/shard_map/mul | solution.py:188
  1651.0 21.4 %copy.487 = f32[343,64,165]{0,1,2:T(8,128)} copy(f32[343,64,165]{2,1,0:T(8,128)} %broadcast_multiply_fusion.14) | data formatting | bytes 28976640 | tf_op jit(solution)/shard_map/mul | solution.py:188
  1672.5 53.1 %fusion.9 = f32[64,165,1]{1,0,2:T(8,128)S(1)} fusion(f32[343,64,165]{0,1,2:T(8,128)} %copy.487, f32[343,165,165]{0,2,1:T(8,128)} %get-tuple-element.798), kind=kOutput, calls=%fused_computation.205 | convolution fusion | flops 7171718144 | bytes 51883260 | tf_op jit(solution)/shard_map/vcm,vjm->cj/dot_general | solution.py:190
  1725.6 6.6 fusion.11
  1732.2 6.6 fusion.13
  (1129 shorter events, 150.7 us)
Async XLA Ops:
  19.6 51.8 %copy-start.5 = (f32[8,165,165,1,1]{2,1,0,4,3:T(8,128)S(1)}, f32[8,165,165,1,1]{2,1,0,4,3:T(8,128)}, u32[]{:S(2)}) copy-start(f32[8,165,165,1,1]{2,1,0,4,3:T(8,128)} %constant.239) | copy-start | bytes 2613604
  28.2 89.1 %copy-start.13 = (f32[64,1,165]{2,0,1:T(8,128)}, f32[64,1,165]{2,0,1:T(8,128)S(1)}, u32[]{:S(2)}) copy-start(f32[64,1,165]{2,0,1:T(8,128)S(1)} %copy.563) | copy-start | bytes 126724
  28.9 1428.6 %collective-permute-start.6 = (f32[3,4,4,165]{3,2,1,0:T(4,128)}, f32[3,4,4,165]{3,2,1,0:T(4,128)}, u32[]{:S(2)}, u32[]{:S(2)}) collective-permute-start(f32[3,4,4,165]{3,2,1,0:T(4,128)} %slice.894), channel_id=1, source_target_pairs={{0,8},{8,16},{16,24},{1,9},{9,17},{17,25},{2,10},{10,18},{18,26},{... | collective-permute-start | bytes 95048 | tf_op jit(solution)/shard_map/ppermute | solution.py:22
  32.6 1425.6 %collective-permute-start.7 = (f32[3,4,4,165]{3,2,1,0:T(4,128)}, f32[3,4,4,165]{3,2,1,0:T(4,128)}, u32[]{:S(2)}, u32[]{:S(2)}) collective-permute-start(f32[3,4,4,165]{3,2,1,0:T(4,128)} %slice.896), channel_id=1, source_target_pairs={{8,0},{16,8},{24,16},{9,1},{17,9},{25,17},{10,2},{18,10},{26,18},{... | collective-permute-start | bytes 95048 | tf_op jit(solution)/shard_map/ppermute | solution.py:23
  36.5 1425.3 %collective-permute-start = (f32[4,1,4,4,128]{4,3,2,1,0:T(4,128)}, f32[4,1,4,4,128]{4,3,2,1,0:T(4,128)}, u32[]{:S(2)}, u32[]{:S(2)}) collective-permute-start(f32[4,1,4,4,128]{4,3,2,1,0:T(4,128)} %get-tuple-element.810), channel_id=1, source_target_pairs={{0,8},{8,16},{16,24},{1,9},{9,17},{17,25},{2,10},{10,18},{18,26},{... | collective-permute-start | bytes 98312 | tf_op jit(solution)/shard_map/ppermute | solution.py:22
  39.3 1422.5 %collective-permute-start.1 = (f32[4,1,4,4,128]{4,3,2,1,0:T(4,128)}, f32[4,1,4,4,128]{4,3,2,1,0:T(4,128)}, u32[]{:S(2)}, u32[]{:S(2)}) collective-permute-start(f32[4,1,4,4,128]{4,3,2,1,0:T(4,128)} %get-tuple-element.811), channel_id=1, source_target_pairs={{8,0},{16,8},{24,16},{9,1},{17,9},{25,17},{10,2},{18,10},{26,18},{... | collective-permute-start | bytes 98312 | tf_op jit(solution)/shard_map/ppermute | solution.py:23
  209.7 36.3 %copy-start.123 = (f32[1,343]{1,0:T(1,128)S(1)}, f32[1,343]{1,0:T(1,128)}, u32[]{:S(2)}) copy-start(f32[1,343]{1,0:T(1,128)} %get-tuple-element.449) | copy-start | bytes 4120
  209.7 36.3 %copy-start.23 = (f32[1,343]{1,0:T(1,128)S(1)}, f32[1,343]{1,0:T(1,128)}, u32[]{:S(2)}) copy-start(f32[1,343]{1,0:T(1,128)} %copy-done.22) | copy-start | bytes 4120
  209.8 36.3 %copy-start.25 = (f32[1,343]{1,0:T(1,128)S(1)}, f32[1,343]{1,0:T(1,128)}, u32[]{:S(2)}) copy-start(f32[1,343]{1,0:T(1,128)} %copy-done.24) | copy-start | bytes 4120
  209.8 36.3 %copy-start.134 = (f32[1,343]{1,0:T(1,128)S(1)}, f32[1,343]{1,0:T(1,128)}, u32[]{:S(2)}) copy-start(f32[1,343]{1,0:T(1,128)} %get-tuple-element.464) | copy-start | bytes 4120
  209.8 36.3 %copy-start.135 = (f32[1,343]{1,0:T(1,128)S(1)}, f32[1,343]{1,0:T(1,128)}, u32[]{:S(2)}) copy-start(f32[1,343]{1,0:T(1,128)} %get-tuple-element.465) | copy-start | bytes 4120
  209.8 36.3 %copy-start.136 = (f32[1,343]{1,0:T(1,128)S(1)}, f32[1,343]{1,0:T(1,128)}, u32[]{:S(2)}) copy-start(f32[1,343]{1,0:T(1,128)} %get-tuple-element.466) | copy-start | bytes 4120
  209.8 36.3 %copy-start.150 = (f32[1,343]{1,0:T(1,128)S(1)}, f32[1,343]{1,0:T(1,128)}, u32[]{:S(2)}) copy-start(f32[1,343]{1,0:T(1,128)} %get-tuple-element.463) | copy-start | bytes 4120
  209.8 36.5 %copy-start.122 = (f32[1,343]{1,0:T(1,128)S(1)}, f32[1,343]{1,0:T(1,128)}, u32[]{:S(2)}) copy-start(f32[1,343]{1,0:T(1,128)} %get-tuple-element.402) | copy-start | bytes 4120
  209.8 36.6 %copy-start.64 = (f32[1,343]{1,0:T(1,128)S(1)}, f32[1,343]{1,0:T(1,128)}, u32[]{:S(2)}) copy-start(f32[1,343]{1,0:T(1,128)} %get-tuple-element.368) | copy-start | bytes 4120
  209.8 36.6 %copy-start.65 = (f32[1,343]{1,0:T(1,128)S(1)}, f32[1,343]{1,0:T(1,128)}, u32[]{:S(2)}) copy-start(f32[1,343]{1,0:T(1,128)} %get-tuple-element.369) | copy-start | bytes 4120
  209.8 36.6 %copy-start.66 = (f32[1,343]{1,0:T(1,128)S(1)}, f32[1,343]{1,0:T(1,128)}, u32[]{:S(2)}) copy-start(f32[1,343]{1,0:T(1,128)} %get-tuple-element.370) | copy-start | bytes 4120
  209.8 36.6 %copy-start.149 = (f32[1,343]{1,0:T(1,128)S(1)}, f32[1,343]{1,0:T(1,128)}, u32[]{:S(2)}) copy-start(f32[1,343]{1,0:T(1,128)} %get-tuple-element.367) | copy-start | bytes 4120
  209.8 36.9 %copy-start.37 = (f32[1,343]{1,0:T(1,128)S(1)}, f32[1,343]{1,0:T(1,128)}, u32[]{:S(2)}) copy-start(f32[1,343]{1,0:T(1,128)} %copy-done.36) | copy-start | bytes 4120
  209.9 36.9 %copy-start.39 = (f32[1,343]{1,0:T(1,128)S(1)}, f32[1,343]{1,0:T(1,128)}, u32[]{:S(2)}) copy-start(f32[1,343]{1,0:T(1,128)} %copy-done.38) | copy-start | bytes 4120
  209.9 36.9 %copy-start.41 = (f32[1,343]{1,0:T(1,128)S(1)}, f32[1,343]{1,0:T(1,128)}, u32[]{:S(2)}) copy-start(f32[1,343]{1,0:T(1,128)} %copy-done.40) | copy-start | bytes 4120
  209.9 36.9 %copy-start.43 = (f32[1,343]{1,0:T(1,128)S(1)}, f32[1,343]{1,0:T(1,128)}, u32[]{:S(2)}) copy-start(f32[1,343]{1,0:T(1,128)} %copy-done.42) | copy-start | bytes 4120
  209.9 36.9 %copy-start.45 = (f32[1,343]{1,0:T(1,128)S(1)}, f32[1,343]{1,0:T(1,128)}, u32[]{:S(2)}) copy-start(f32[1,343]{1,0:T(1,128)} %copy-done.44) | copy-start | bytes 4120
  209.9 36.9 %copy-start.47 = (f32[1,343]{1,0:T(1,128)S(1)}, f32[1,343]{1,0:T(1,128)}, u32[]{:S(2)}) copy-start(f32[1,343]{1,0:T(1,128)} %copy-done.46) | copy-start | bytes 4120
  209.9 36.9 %copy-start.98 = (f32[1,343]{1,0:T(1,128)S(1)}, f32[1,343]{1,0:T(1,128)}, u32[]{:S(2)}) copy-start(f32[1,343]{1,0:T(1,128)} %copy-done.97) | copy-start | bytes 4120
  209.9 36.9 %copy-start.100 = (f32[1,343]{1,0:T(1,128)S(1)}, f32[1,343]{1,0:T(1,128)}, u32[]{:S(2)}) copy-start(f32[1,343]{1,0:T(1,128)} %copy-done.99) | copy-start | bytes 4120
  209.9 36.9 %copy-start.111 = (f32[1,343]{1,0:T(1,128)S(1)}, f32[1,343]{1,0:T(1,128)}, u32[]{:S(2)}) copy-start(f32[1,343]{1,0:T(1,128)} %copy-done.110) | copy-start | bytes 4120
  209.9 36.9 %copy-start.113 = (f32[1,343]{1,0:T(1,128)S(1)}, f32[1,343]{1,0:T(1,128)}, u32[]{:S(2)}) copy-start(f32[1,343]{1,0:T(1,128)} %copy-done.112) | copy-start | bytes 4120
  209.9 36.9 %copy-start.115 = (f32[1,343]{1,0:T(1,128)S(1)}, f32[1,343]{1,0:T(1,128)}, u32[]{:S(2)}) copy-start(f32[1,343]{1,0:T(1,128)} %copy-done.114) | copy-start | bytes 4120
  210.0 36.9 %copy-start.117 = (f32[1,343]{1,0:T(1,128)S(1)}, f32[1,343]{1,0:T(1,128)}, u32[]{:S(2)}) copy-start(f32[1,343]{1,0:T(1,128)} %copy-done.116) | copy-start | bytes 4120
  210.0 36.9 %copy-start.119 = (f32[1,343]{1,0:T(1,128)S(1)}, f32[1,343]{1,0:T(1,128)}, u32[]{:S(2)}) copy-start(f32[1,343]{1,0:T(1,128)} %copy-done.118) | copy-start | bytes 4120
  210.0 36.9 %copy-start.121 = (f32[1,343]{1,0:T(1,128)S(1)}, f32[1,343]{1,0:T(1,128)}, u32[]{:S(2)}) copy-start(f32[1,343]{1,0:T(1,128)} %copy-done.120) | copy-start | bytes 4120
  210.0 36.9 %copy-start.140 = (f32[1,343]{1,0:T(1,128)S(1)}, f32[1,343]{1,0:T(1,128)}, u32[]{:S(2)}) copy-start(f32[1,343]{1,0:T(1,128)} %copy-done.139) | copy-start | bytes 4120
  210.0 36.9 %copy-start.148 = (f32[1,343]{1,0:T(1,128)S(1)}, f32[1,343]{1,0:T(1,128)}, u32[]{:S(2)}) copy-start(f32[1,343]{1,0:T(1,128)} %copy-done.147) | copy-start | bytes 4120
  210.0 36.9 %copy-start.152 = (f32[1,343]{1,0:T(1,128)S(1)}, f32[1,343]{1,0:T(1,128)}, u32[]{:S(2)}) copy-start(f32[1,343]{1,0:T(1,128)} %get-tuple-element.898) | copy-start | bytes 4120
  210.0 36.9 %copy-start.153 = (f32[1,343]{1,0:T(1,128)S(1)}, f32[1,343]{1,0:T(1,128)}, u32[]{:S(2)}) copy-start(f32[1,343]{1,0:T(1,128)} %get-tuple-element.906) | copy-start | bytes 4120
  210.0 36.9 %copy-start.154 = (f32[1,343]{1,0:T(1,128)S(1)}, f32[1,343]{1,0:T(1,128)}, u32[]{:S(2)}) copy-start(f32[1,343]{1,0:T(1,128)} %get-tuple-element.353) | copy-start | bytes 4120
  210.0 36.9 %copy-start.155 = (f32[1,343]{1,0:T(1,128)S(1)}, f32[1,343]{1,0:T(1,128)}, u32[]{:S(2)}) copy-start(f32[1,343]{1,0:T(1,128)} %get-tuple-element.388) | copy-start | bytes 4120
  210.1 36.9 %copy-start.156 = (f32[1,343]{1,0:T(1,128)S(1)}, f32[1,343]{1,0:T(1,128)}, u32[]{:S(2)}) copy-start(f32[1,343]{1,0:T(1,128)} %get-tuple-element.415) | copy-start | bytes 4120
  210.1 36.9 %copy-start.157 = (f32[1,343]{1,0:T(1,128)S(1)}, f32[1,343]{1,0:T(1,128)}, u32[]{:S(2)}) copy-start(f32[1,343]{1,0:T(1,128)} %get-tuple-element.360) | copy-start | bytes 4120
  210.1 36.9 %copy-start.158 = (f32[1,343]{1,0:T(1,128)S(1)}, f32[1,343]{1,0:T(1,128)}, u32[]{:S(2)}) copy-start(f32[1,343]{1,0:T(1,128)} %get-tuple-element.442) | copy-start | bytes 4120
  210.1 36.9 %copy-start.159 = (f32[1,343]{1,0:T(1,128)S(1)}, f32[1,343]{1,0:T(1,128)}, u32[]{:S(2)}) copy-start(f32[1,343]{1,0:T(1,128)} %get-tuple-element.401) | copy-start | bytes 4120
  318.4 36.3 %copy-start.162 = (f32[16,2,1]{0,1,2:T(2,128)S(1)}, f32[16,2,1]{0,1,2:T(2,128)}, u32[]{:S(2)}) copy-start(f32[16,2,1]{0,1,2:T(2,128)} %multiply_add_fusion.5) | copy-start | bytes 388
  318.4 36.4 %copy-start.12 = (f32[8,165,165,1]{2,1,0,3:T(8,128)S(1)}, f32[8,165,165,1]{2,1,0,3:T(8,128)}, u32[]{:S(2)}) copy-start(f32[8,165,165,1]{2,1,0,3:T(8,128)} %constant.240) | copy-start | bytes 2613604
  318.4 36.4 %copy-start.15 = (f32[16,2,8,165]{3,2,1,0:T(8,128)S(1)}, f32[16,2,8,165]{3,2,1,0:T(8,128)}, u32[]{:S(2)}) copy-start(f32[16,2,8,165]{3,2,1,0:T(8,128)} %dot_general.58) | copy-start | bytes 506884
  318.5 37.9 %copy-start.4 = (f32[165,165]{1,0:T(8,128)S(1)}, f32[165,165]{1,0:T(8,128)}, u32[]{:S(2)}) copy-start(f32[165,165]{1,0:T(8,128)} %constant.217.clone) | copy-start | bytes 326704
  318.5 37.8 %copy-start.8 = (s32[27225]{0:T(1024)S(1)}, s32[27225]{0:T(1024)}, u32[]{:S(2)}) copy-start(s32[27225]{0:T(1024)} %constant.232) | copy-start | bytes 326704
  318.5 37.8 %copy-start.73 = (f32[165]{0:T(256)S(1)}, f32[165]{0:T(256)}, u32[]{:S(2)}) copy-start(f32[165]{0:T(256)} %custom-call) | copy-start | bytes 1984
  1343.1 57.8 %copy-start.11 = (f32[2,2,2,165,165]{4,3,2,1,0:T(8,128)S(1)}, f32[2,2,2,165,165]{4,3,2,1,0:T(8,128)}, u32[]{:S(2)}) copy-start(f32[2,2,2,165,165]{4,3,2,1,0:T(8,128)} %constant.227) | copy-start | bytes 2613604
  1343.1 59.0 %copy-start.1 = (f32[8,165,343]{2,1,0:T(8,128)S(1)}, f32[8,165,343]{2,1,0:T(8,128)}, u32[]{:S(2)}) copy-start(f32[8,165,343]{2,1,0:T(8,128)} %copy.493) | copy-start | bytes 5433124
  1402.2 52.6 %copy-start.6 = (f32[8,165,165,1,1]{2,1,0,4,3:T(8,128)S(1)}, f32[8,165,165,1,1]{2,1,0,4,3:T(8,128)}, u32[]{:S(2)}) copy-start(f32[8,165,165,1,1]{2,1,0,4,3:T(8,128)} %constant.239) | copy-start | bytes 2613604
  1402.2 53.4 %copy-start.163 = (s32[4]{0:T(128)S(1)}, s32[4]{0:T(128)}, u32[]{:S(2)}) copy-start(s32[4]{0:T(128)} %and_select_fusion.2) | copy-start | bytes 52
  1402.2 55.0 %copy-start.161 = (pred[343]{0:T(512)(128)(4,1)S(1)}, pred[343]{0:T(512)(128)(4,1)}, u32[]{:S(2)}) copy-start(pred[343]{0:T(512)(128)(4,1)} %copy-done.160) | copy-start | bytes 1033
  1402.2 55.0 %copy-start.14 = (f32[64,1,165]{2,0,1:T(8,128)S(1)}, f32[64,1,165]{2,0,1:T(8,128)}, u32[]{:S(2)}) copy-start(f32[64,1,165]{2,0,1:T(8,128)} %copy-done.13) | copy-start | bytes 126724
  1402.2 59.6 %copy-start.3 = (f32[3,4,4,4,128]{4,3,2,1,0:T(4,128)S(1)}, f32[3,4,4,4,128]{4,3,2,1,0:T(4,128)}, u32[]{:S(2)}) copy-start(f32[3,4,4,4,128]{4,3,2,1,0:T(4,128)} %param.16) | copy-start | bytes 294916
  1402.2 59.6 %copy-start.10 = (f32[1,4,4,4,128]{4,3,2,1,0:T(4,128)S(1)}, f32[1,4,4,4,128]{4,3,2,1,0:T(4,128)}, u32[]{:S(2)}) copy-start(f32[1,4,4,4,128]{4,3,2,1,0:T(4,128)} %copy-done.9) | copy-start | bytes 98308
  1459.1 19.4 %collective-permute-start.8 = (f32[10,3,4,165]{3,2,1,0:T(4,128)S(1)}, f32[10,3,4,165]{3,2,1,0:T(4,128)S(1)}, u32[]{:S(2)}, u32[]{:S(2)}) collective-permute-start(f32[10,3,4,165]{3,2,1,0:T(4,128)S(1)} %get-tuple-element.800), channel_id=1, source_target_pairs={{0,2},{2,4},{4,6},{1,3},{3,5},{5,7},{8,10},{10,12},{12,14},{9,11},... | collective-permute-start | bytes 237608 | tf_op jit(solution)/shard_map/ppermute | solution.py:22
  1460.4 18.1 %collective-permute-start.9 = (f32[10,3,4,165]{3,2,1,0:T(4,128)S(1)}, f32[10,3,4,165]{3,2,1,0:T(4,128)S(1)}, u32[]{:S(2)}, u32[]{:S(2)}) collective-permute-start(f32[10,3,4,165]{3,2,1,0:T(4,128)S(1)} %get-tuple-element.801), channel_id=1, source_target_pairs={{2,0},{4,2},{6,4},{3,1},{5,3},{7,5},{10,8},{12,10},{14,12},{11,9},... | collective-permute-start | bytes 237608 | tf_op jit(solution)/shard_map/ppermute | solution.py:23
  1462.6 6.9 collective-permute-start.2
  1466.6 4.8 collective-permute-start.3
  1472.4 10.9 collective-permute-start.4
  1473.7 9.6 collective-permute-start.5
  1478.9 91.5 %collective-permute-start.10 = (f32[10,10,3,165]{3,2,1,0:T(4,128)S(1)}, f32[10,10,3,165]{3,2,1,0:T(4,128)S(1)}, u32[]{:S(2)}, u32[]{:S(2)}) collective-permute-start(f32[10,10,3,165]{3,2,1,0:T(4,128)S(1)} %get-tuple-element.764), channel_id=1, source_target_pairs={{0,1},{2,3},{4,5},{6,7},{8,9},{10,11},{12,13},{14,15},{16,17},{18,... | collective-permute-start | bytes 594008 | tf_op jit(solution)/shard_map/ppermute | solution.py:22
  1480.2 90.2 %collective-permute-start.11 = (f32[10,10,3,165]{3,2,1,0:T(4,128)S(1)}, f32[10,10,3,165]{3,2,1,0:T(4,128)S(1)}, u32[]{:S(2)}, u32[]{:S(2)}) collective-permute-start(f32[10,10,3,165]{3,2,1,0:T(4,128)S(1)} %get-tuple-element.765), channel_id=1, source_target_pairs={{1,0},{3,2},{5,4},{7,6},{9,8},{11,10},{13,12},{15,14},{17,16},{19,... | collective-permute-start | bytes 594008 | tf_op jit(solution)/shard_map/ppermute | solution.py:23
  (112 other events, 904.3 us)
where the time goes:
time: 1750 us; the launch traced here: 1740 us
  local copies, waits for them, and re-layouts  1280 us (73%)
  other arithmetic  227 us (13%)
  matrix products  153 us (9%)
  blocking collectives  43 us (2%)
  starting transfers between devices  29.7 us (2%)
    gather x48, local copies, waits for them, and re-layouts, add_block(): kernel = terms[source_index] * weight_table[:, :, None]  947 us
    gather x4, local copies, waits for them, and re-layouts, window_kernel(): kernel = terms[source_index] * weights[:, :, None]  207 us
    dot_general x2, matrix products, window_interactions(): result = jnp.einsum('vcm,vjm->cj', gathered, kernel, precision=HIGHEST)  106 us
    reduce_sum x7, other arithmetic, near_field(): jnp.sum(source[3][..., None, :] / jnp.sqrt(squared), axis=-1)  84.6 us
    mul x1, other arithmetic, window_kernel(): kernel = terms[source_index] * weights[:, :, None]  57.8 us
    div x469, other arithmetic, taylor_terms(): -((2 * degree - 1) * linear_part + (degree - 1) * square_part)  45.2 us
    all_gather x1, blocking collectives, shards(): lax.all_gather(moments1[None], ('gx', 'gy', 'gz'), axis=0, tiled=True)  43 us
  transfers between devices with their start and end apart: 12, of which 1 were waited for; matrix products, arithmetic and copies ran while one was open for 84% of the time, Pallas kernels for 0%

commit v1 on v0

v1 whole, which is shorter than its diff:
```python
import functools
import math

import jax
import jax.numpy as jnp
import ml_dtypes
import numpy as np
from jax import lax
from jax.experimental import pallas as pl
from jax.experimental.pallas import tpu as pltpu
from jax.sharding import PartitionSpec as P

ORDER = 8
SOFTENING = 0.02
HIGHEST = lax.Precision.HIGHEST
LANES = 128
ROWS = 16
VMEM_BYTES = 48 * 1024 * 1024


def multi_indices():
    listed = []
    for degree in range(ORDER + 1):
        for first in range(degree, -1, -1):
            for second in range(degree - first, -1, -1):
                listed.append((first, second, degree - first - second))
    return listed


FULL = multi_indices()
BASIS = [n for n in FULL if n[2] <= 1]
SLOT = {n: i for i, n in enumerate(BASIS)}
TERMS = len(BASIS)


def fold_row(n):
    w = n[2] // 2
    return [
        (SLOT[(n[0] + 2 * u, n[1] + 2 * (w - u), n[2] - 2 * w)], (-1.0) ** w * math.comb(w, u))
        for u in range(w + 1)
    ]


def derivatives(vectors):
    r = [vectors[:, i] for i in range(3)]
    sq = r[0] ** 2 + r[1] ** 2 + r[2] ** 2
    a = {(0, 0, 0): 1.0 / np.sqrt(sq)}
    for n in FULL[1:]:
        d = sum(n)
        lin = np.zeros_like(sq)
        two = np.zeros_like(sq)
        for i in range(3):
            low = list(n)
            low[i] -= 1
            if low[i] >= 0:
                lin = lin + r[i] * a[tuple(low)]
            low[i] -= 1
            if low[i] >= 0:
                two = two + a[tuple(low)]
        a[n] = -((2 * d - 1) * lin + (d - 1) * two) / (d * sq)
    return {n: a[n] * math.prod(math.factorial(c) for c in n) for n in FULL}


def translation(offsets):
    offsets = np.asarray(offsets, np.float64)
    near = np.max(np.abs(offsets), axis=1) <= 1.5
    b = derivatives(np.where(near[:, None], [4.0, 0.0, 0.0], -offsets))
    out = np.zeros((len(offsets), LANES, LANES))
    for h, hn in enumerate(BASIS):
        for j, jn in enumerate(BASIS):
            n = tuple(hn[i] + jn[i] for i in range(3))
            if sum(n) <= ORDER:
                out[:, h, j] = np.where(near, 0.0, b[n])
    return out


def power_ratio(u, k):
    if min(k) < 0:
        return 0.0
    return math.prod(u[i] ** k[i] / math.factorial(k[i]) for i in range(3))


@functools.lru_cache(None)
def shift_tables():
    up = np.zeros((8, LANES, LANES))
    down = np.zeros((8, LANES, LANES))
    for g in range(8):
        u = [(g >> 2 & 1) - 0.5, (g >> 1 & 1) - 0.5, (g & 1) - 0.5]
        for n in FULL:
            scale = 0.5 ** sum(n)
            for h, coefficient in fold_row(n):
                for i, k in enumerate(BASIS):
                    gap = tuple(n[d] - k[d] for d in range(3))
                    up[g, i, h] += scale * coefficient * power_ratio([-c for c in u], gap)
                    down[g, h, i] += scale * coefficient * power_ratio(u, gap)
    return (
        up.reshape(8 * LANES, LANES).astype(np.float32),
        down.transpose(1, 0, 2).reshape(LANES, 8 * LANES).astype(np.float32),
    )


@functools.lru_cache(None)
def window_table():
    grid = [(x - 3, y - 3, z - 3) for x in range(7) for y in range(7) for z in range(7)]
    table = translation(grid).reshape(49, 7 * LANES, LANES).astype(np.float32)
    high = table.astype(ml_dtypes.bfloat16)
    low = (table - high.astype(np.float32)).astype(ml_dtypes.bfloat16)
    return np.concatenate([high, low], axis=-1)


@functools.lru_cache(None)
def top_table(shape):
    grid = [
        (x, y, z)
        for x in range(1 - shape[0], shape[0])
        for y in range(1 - shape[1], shape[1])
        for z in range(1 - shape[2], shape[2])
    ]
    table = translation(grid)[:, :, :]
    return table.reshape(tuple(2 * s - 1 for s in shape) + (LANES, LANES)).astype(np.float32)


def harmonics(position):
    ladders = []
    for d in range(3):
        rungs = [jnp.ones_like(position[d])]
        for step in range(1, ORDER + 1):
            rungs.append(rungs[-1] * position[d] * (1.0 / step))
        ladders.append(rungs)
    flat = {
        (a, b): ladders[0][a] * ladders[1][b] for a in range(ORDER + 1) for b in range(ORDER + 1 - a)
    }
    found = []
    for a, b, c in BASIS:
        total = None
        for w in range(a // 2 + b // 2 + 1):
            inner = None
            for u in range(w + 1):
                v = w - u
                if 2 * u <= a and 2 * v <= b:
                    term = flat[(a - 2 * u, b - 2 * v)]
                    factor = (-1.0) ** w * math.comb(w, u)
                    term = term if factor == 1.0 else term * factor
                    inner = term if inner is None else inner + term
            if inner is not None:
                part = inner * ladders[2][c + 2 * w]
                total = part if total is None else total + part
        found.append(total)
    return found


def moment_kernel(position_ref, charge_ref, out_ref):
    charge = charge_ref[...]
    values = harmonics([position_ref[d] - 0.5 for d in range(3)])
    lane = lax.broadcasted_iota(jnp.int32, (8, LANES), 1)
    total = jnp.zeros((8, LANES), jnp.float32)
    for h, n in enumerate(BASIS):
        summed = jnp.sum(values[h] * charge, axis=1, keepdims=True)
        if sum(n) % 2:
            summed = -summed
        total = jnp.where(lane == h, summed, total)
    out_ref[...] = total


def leaf_moments(offsets, charge):
    tiles, slots = charge.shape
    return pl.pallas_call(
        moment_kernel,
        grid=(tiles // 8,),
        out_shape=jax.ShapeDtypeStruct((tiles, LANES), jnp.float32),
        in_specs=[
            pl.BlockSpec((3, 8, slots), lambda i: (0, i, 0)),
            pl.BlockSpec((8, slots), lambda i: (i, 0)),
        ],
        out_specs=pl.BlockSpec((8, LANES), lambda i: (i, 0)),
        compiler_params=pltpu.CompilerParams(vmem_limit_bytes=VMEM_BYTES),
    )(offsets, charge)


def evaluate_kernel(position_ref, charge_ref, live_ref, near_ref, total_ref, leaf_ref, full_ref, part_ref, far_ref):
    live = live_ref[...]
    values = harmonics([position_ref[d] - 0.5 for d in range(3)])
    total, leaf = total_ref[...], leaf_ref[...]
    far = jnp.zeros_like(live)
    local = jnp.zeros_like(live)
    for h in range(TERMS):
        far = far + values[h] * total[:, h : h + 1]
        local = local + values[h] * leaf[:, h : h + 1]
    near = jnp.where(live > 0.0, near_ref[...] - charge_ref[...] / SOFTENING, 0.0)
    full_ref[...] = -(near + far) * live
    part_ref[...] = -near * live
    far_ref[...] = -local * live


def evaluate(offsets, charge, live, near, total, leaf):
    tiles, slots = charge.shape
    row = pl.BlockSpec((8, slots), lambda i: (i, 0))
    shape = jax.ShapeDtypeStruct((tiles, slots), jnp.float32)
    return pl.pallas_call(
        evaluate_kernel,
        grid=(tiles // 8,),
        out_shape=(shape, shape, shape),
        in_specs=[pl.BlockSpec((3, 8, slots), lambda i: (0, i, 0)), row, row, row, row, row],
        out_specs=(row, row, row),
        compiler_params=pltpu.CompilerParams(vmem_limit_bytes=VMEM_BYTES),
    )(offsets, charge, live, near, total, leaf)


def near_kernel(extents, counts_ref, window_ref, out_ref, columns_ref, sums_ref):
    lx, ly, lz = extents

    def one_leaf(leaf, carry):
        x = leaf // (ly * lz)
        y = lax.rem(leaf // lz, ly)
        z = lax.rem(leaf, lz)

        def cell(p, q, r):
            return ((x + p) * (ly + 2) + y + q) * (lz + 2) + z + r

        columns_ref[...] = jnp.transpose(window_ref[cell(1, 1, 1)])

        def one_chunk(chunk, inner):
            start = pl.multiple_of(chunk * ROWS, ROWS)
            target = columns_ref[pl.ds(start, ROWS), :]
            wide = [jnp.broadcast_to(target[:, d : d + 1], (ROWS, LANES)) for d in range(3)]
            moved = [[wide[d] - float(s - 1) for s in range(3)] for d in range(3)]
            total = jnp.zeros((ROWS, LANES), jnp.float32)
            for p in range(3):
                for q in range(3):
                    for r in range(3):
                        index = cell(p, q, r)
                        gx = window_ref[index, 0:1, :] - moved[0][p]
                        gy = window_ref[index, 1:2, :] - moved[1][q]
                        gz = window_ref[index, 2:3, :] - moved[2][r]
                        squared = (gx * gx + SOFTENING * SOFTENING) + (gy * gy + gz * gz)
                        total = total + window_ref[index, 3:4, :] * lax.rsqrt(squared)
            sums_ref[pl.ds(start, ROWS), :] = total
            return inner

        lax.fori_loop(0, (counts_ref[leaf] + ROWS - 1) // ROWS, one_chunk, 0)
        out_ref[pl.ds(leaf, 1), :] = jnp.sum(jnp.transpose(sums_ref[...]), axis=0, keepdims=True)
        return carry

    lax.fori_loop(0, lx * ly * lz, one_leaf, 0)


def near_field(window, counts, extents):
    tiles = extents[0] * extents[1] * extents[2]
    return pl.pallas_call(
        functools.partial(near_kernel, extents),
        out_shape=jax.ShapeDtypeStruct((tiles, LANES), jnp.float32),
        in_specs=[
            pl.BlockSpec(memory_space=pltpu.SMEM),
            pl.BlockSpec(memory_space=pltpu.VMEM),
        ],
        out_specs=pl.BlockSpec(memory_space=pltpu.VMEM),
        scratch_shapes=[
            pltpu.VMEM((LANES, 8), jnp.float32),
            pltpu.VMEM((LANES, LANES), jnp.float32),
        ],
        compiler_params=pltpu.CompilerParams(vmem_limit_bytes=VMEM_BYTES),
    )(counts, window)


def local_kernel(lx, plane, small, leaf_ref, mid_ref, table_ref, out_ref, acc_ref):
    step = pl.program_id(0)
    dx, dy = step // 7, lax.rem(step, 7)
    rows = lx * plane
    depth = 7 * LANES

    @pl.when(step == 0)
    def _():
        acc_ref[...] = jnp.zeros_like(acc_ref)

    leaf = leaf_ref[dy, pl.ds(dx, lx)].reshape(rows, depth)
    odd = lax.rem(lax.broadcasted_iota(jnp.int32, (rows, depth), 0) // plane, 2)
    drop = jnp.where(dx == 0, 0, jnp.where(dx == 6, 1, 2))
    leaf = jnp.where(odd == drop, 0.0, leaf)
    whole = jnp.concatenate([leaf, mid_ref[0]], axis=0)
    high = whole.astype(jnp.bfloat16).astype(jnp.float32)
    both = jnp.concatenate([high, whole - high], axis=0).astype(jnp.bfloat16)
    acc_ref[...] += jnp.dot(both, table_ref[0], preferred_element_type=jnp.float32)

    @pl.when(step == 48)
    def _():
        cut = rows + small
        out_ref[...] = (
            acc_ref[:cut, :LANES] + acc_ref[:cut, LANES:] + acc_ref[cut:, :LANES]
        )


def local_expansions(leaf, mid, table):
    lx, plane, depth = leaf.shape[1] - 6, leaf.shape[2], leaf.shape[3]
    small = mid.shape[1]
    rows = lx * plane + small
    return pl.pallas_call(
        functools.partial(local_kernel, lx, plane, small),
        grid=(49,),
        out_shape=jax.ShapeDtypeStruct((rows, LANES), jnp.float32),
        in_specs=[
            pl.BlockSpec(memory_space=pltpu.VMEM),
            pl.BlockSpec((1, small, depth), lambda i: (i, 0, 0)),
            pl.BlockSpec((1, depth, 2 * LANES), lambda i: (i, 0, 0)),
        ],
        out_specs=pl.BlockSpec((rows, LANES), lambda i: (0, 0)),
        scratch_shapes=[pltpu.VMEM((2 * rows, 2 * LANES), jnp.float32)],
        compiler_params=pltpu.CompilerParams(vmem_limit_bytes=VMEM_BYTES),
    )(leaf, mid, table)


def with_halo(shard, sides, width):
    for axis, dim in sides:
        peers, length = (lax.axis_size(axis), shard.shape[dim])
        up = [(i, (i + 1) % peers) for i in range(peers - 1)]
        down = [(j, i) for i, j in up]
        before = lax.ppermute(lax.slice_in_dim(shard, length - width, length, axis=dim), axis, up)
        after = lax.ppermute(lax.slice_in_dim(shard, 0, width, axis=dim), axis, down)
        shard = jnp.concatenate([before, shard, after], axis=dim)
    return shard


def gather_axis(piece, axis):
    peers, me = lax.axis_size(axis), lax.axis_index(axis)
    whole = jnp.zeros((peers,) + piece.shape, piece.dtype)
    rest = (0,) * piece.ndim
    whole = lax.dynamic_update_slice(whole, piece[None], (me,) + rest)
    for step in range(1, peers):
        came = lax.ppermute(piece, axis, [(i, (i + step) % peers) for i in range(peers)])
        whole = lax.dynamic_update_slice(whole, came[None], (lax.rem(me + peers - step, peers),) + rest)
    return whole


def kept(length, shift):
    cells = np.arange(length)
    return (np.abs((cells + shift - 3) // 2 - cells // 2) <= 1).astype(np.float32)


def side_by_side(window, length):
    return jnp.concatenate(
        [window[:, :, s : s + length] * kept(length, s)[:, None] for s in range(7)], axis=-1
    )


def group(moments):
    a, b, c, n = moments.shape
    paired = moments.reshape(a // 2, 2, b // 2, 2, c // 2, 2, n).transpose(0, 2, 4, 1, 3, 5, 6)
    return paired.reshape(a * b * c // 8, 8 * n)


def spread(parents, extents):
    a, b, c = extents
    apart = parents.reshape(a, b, c, 2, 2, 2, LANES).transpose(0, 3, 1, 4, 2, 5, 6)
    return apart.reshape(8 * a * b * c, LANES)


def shards(offsets, masses, counts):
    lx, ly, lz = counts.shape
    slots = masses.shape[-1]
    tiles = lx * ly * lz
    live = (jnp.arange(slots, dtype=jnp.int32)[None, None, None, :] < counts[..., None]).astype(
        jnp.float32
    )
    charge = masses * live
    flat_offsets = offsets.reshape(3, tiles, slots)
    flat_charge, flat_live = charge.reshape(tiles, slots), live.reshape(tiles, slots)

    moments0 = leaf_moments(flat_offsets, flat_charge).reshape(lx, ly, lz, LANES)
    up, down = shift_tables()
    mid = (lx // 2, ly // 2, lz // 2)
    top = (lx // 4, ly // 4, lz // 4)
    moments1 = jnp.dot(group(moments0), up, precision=HIGHEST)
    moments2 = jnp.dot(group(moments1.reshape(mid + (LANES,))), up, precision=HIGHEST)
    n_mid, n_top = moments1.shape[0], moments2.shape[0]

    pieces = jnp.concatenate([moments1, moments2], axis=0)
    for axis in ("gz", "gy", "gx"):
        pieces = gather_axis(pieces, axis)
    span = pieces.shape[:3]
    place = tuple(lax.axis_index(axis) for axis in ("gx", "gy", "gz"))

    def whole_grid(part, extents):
        shaped = part.reshape(span + extents + (LANES,)).transpose(0, 3, 1, 4, 2, 5, 6)
        return shaped.reshape(tuple(span[i] * extents[i] for i in range(3)) + (LANES,))

    whole1 = whole_grid(pieces[:, :, :, :n_mid], mid)
    whole2 = whole_grid(pieces[:, :, :, n_mid:], top)

    packed = jnp.stack([offsets[0], offsets[1], offsets[2], charge], axis=3)
    packed = with_halo(packed, (("gx", 0), ("gy", 1), ("gz", 2)), 1)
    packed = jnp.pad(packed, ((0, 0),) * 3 + ((0, 4), (0, 0)))
    near = near_field(packed.reshape(-1, 8, slots), counts.reshape(-1), (lx, ly, lz))

    window0 = with_halo(moments0, (("gx", 0), ("gy", 1), ("gz", 2)), 3)
    lined = side_by_side(window0, lz)
    lined = jnp.stack(
        [lined[:, s : s + ly] * kept(ly, s)[:, None, None] for s in range(7)]
    ).reshape(7, lx + 6, ly * lz, 7 * LANES)
    padded1 = jnp.pad(whole1, ((3, 3), (3, 3), (3, 3), (0, 0)))
    window1 = lax.dynamic_slice(
        padded1,
        tuple(place[i] * mid[i] for i in range(3)) + (0,),
        tuple(mid[i] + 6 for i in range(3)) + (LANES,),
    )
    lined1 = side_by_side(window1, mid[2])
    mids = jnp.stack(
        [
            lined1[s : s + mid[0], t : t + mid[1]]
            * (kept(mid[0], s)[:, None] * kept(mid[1], t)[None, :])[:, :, None, None]
            for s in range(7)
            for t in range(7)
        ]
    ).reshape(49, n_mid, 7 * LANES)
    locals01 = local_expansions(lined, mids, jnp.asarray(window_table()))
    local0, local1 = locals01[:tiles], 0.5 * locals01[tiles:]

    grid2 = whole2.shape[:3]
    table2 = jnp.asarray(top_table(grid2))
    rows2 = []
    for a in range(top[0]):
        for b in range(top[1]):
            for c in range(top[2]):
                start = tuple(
                    grid2[i] - 1 - (place[i] * top[i] + (a, b, c)[i]) for i in range(3)
                )
                used = lax.dynamic_slice(table2, start + (0, 0), grid2 + (LANES, LANES))
                rows2.append(
                    jnp.sum(whole2[..., :, None] * used, axis=(0, 1, 2, 3))
                )
    local2 = 0.25 * jnp.stack(rows2)
    total1 = local1 + spread(jnp.dot(local2, down, precision=HIGHEST), top)
    total0 = local0 + spread(jnp.dot(total1, down, precision=HIGHEST), mid)

    outs = evaluate(flat_offsets, flat_charge, flat_live, near, total0, local0)
    return tuple(out.reshape(lx, ly, lz, slots) for out in outs)


def solution(mesh):
    placed = (P(None, "gx", "gy", "gz", None), P("gx", "gy", "gz", None), P("gx", "gy", "gz"))
    return jax.shard_map(
        shards,
        mesh=mesh,
        in_specs=placed,
        out_specs=(P("gx", "gy", "gz", None),) * 3,
        check_vma=False,
    )
```

time: 1750 us -> 210 us (0.12)
  local copies, waits for them, and re-layouts: 1280 us -> 32.1 us
  other arithmetic: 227 us -> 8.98 us
  matrix products: 153 us -> 2.63 us
  Pallas kernels: 0 us -> 110 us
  blocking collectives: 43 us -> 0 us
    gather x52 -> x0, local copies, waits for them, and re-layouts: 1150 us -> none  [the longest x48 947 us: add_block(): kernel = terms[source_index] * weight_table[:, :, None]]
    dot_general x28 -> x4, matrix products: 153 us -> 2.63 us  [the longest x1 1.39 us: shards(): moments1 = jnp.dot(group(moments0), up, precision=HIGHEST)]
    pallas_call x0 -> x4, Pallas kernels: none -> 110 us  [the longest x1 71.9 us: near_field(): pl.pallas_call(functools.partial(near_kernel, extents), out_shape=jax.Sha...]
    reduce_sum x7 -> x1, other arithmetic: 84.6 us -> 1.94 us  [shards(): rows2.append(jnp.sum(whole2[..., :, None] * used, axis=(0, 1, 2, 3)))]
    mul x20 -> x2, other arithmetic: 78.2 us -> 3.28 us  [the longest x1 1.72 us: shards(): lined[:, s:s + ly] * kept(ly, s)[:, None, None]]
    div x475 -> x0, other arithmetic: 47.1 us -> none  [the longest x469 45.2 us: taylor_terms(): -((2 * degree - 1) * linear_part + (degree - 1) * square_part)]
    all_gather x1 -> x0, blocking collectives: 43 us -> none  [shards(): lax.all_gather(moments1[None], ('gx', 'gy', 'gz'), axis=0, tiled=True)]
    reshape x7 -> x3, local copies, waits for them, and re-layouts: 30.3 us -> 0.08 us  [the longest x2 0.05 us: spread(): parents.reshape(a, b, c, 2, 2, 2, LANES).transpose(0, 3, 1, 4, 2, 5, 6)]
  transfers between devices with their start and end apart: 12 -> 19, of which waited for: 1 -> 4; matrix products, arithmetic and copies ran while one was open for 84% -> 9% of each run, Pallas kernels for 0% -> 35%
where the time goes in v1:
time: 210 us; the launch traced here: 207 us
  Pallas kernels  110 us (52%)
  starting transfers between devices  42.7 us (20%)
  local copies, waits for them, and re-layouts  32.1 us (15%)
  other arithmetic  8.98 us (4%)
  waiting for transfers between devices  7.85 us (4%)
  between operations  2.65 us (1%)
  matrix products  2.63 us (1%)
    pallas_call x1, Pallas kernels, near_field(): pl.pallas_call(functools.partial(near_kernel, extents), out_shape=jax.Sha...  71.9 us
    pallas_call x1, Pallas kernels, local_expansions(): pl.pallas_call(functools.partial(local_kernel, lx, plane, small), grid=(4...  32.7 us
    ppermute x6, starting transfers between devices, with_halo(): lax.ppermute(lax.slice_in_dim(shard, 0, width, axis=dim), axis, down)  20 us
    ppermute x6, starting transfers between devices, with_halo(): lax.ppermute(lax.slice_in_dim(shard, length - width, length, axis=dim), a...  14.9 us
    unnamed x112, local copies, waits for them, and re-layouts  11.7 us
    another operation x8, local copies, waits for them, and re-layouts, shards(): jnp.stack([lined[:, s:s + ly] * kept(ly, s)[:, None, None] for s in range...  10.6 us
    ppermute x7, starting transfers between devices, gather_axis(): lax.ppermute(piece, axis, [(i, (i + step) % peers) for i in range(peers)])  7.84 us
    ppermute x7, waiting for transfers between devices, gather_axis(): lax.ppermute(piece, axis, [(i, (i + step) % peers) for i in range(peers)])  7.81 us
  transfers between devices with their start and end apart: 19, of which 4 were waited for; matrix products, arithmetic and copies ran while one was open for 9% of the time, Pallas kernels for 35%

profile of v1, /device:TPU:5, one launch (start us, length us, event | category | flops | bytes accessed | tf_op | source)
XLA Modules:
  0.0 207.4 jit_solution(11332924280150539684)
XLA Ops:
  0.7 0.9 slice_bitcast_fusion.2
  1.5 0.8 fusion.29
  2.4 3.1 %collective-permute-start.1 = (f32[1,4,4,4,128]{4,2,1,0,3:T(4,128)S(1)}, f32[1,4,4,4,128]{4,2,1,0,3:T(4,128)S(1)}, u32[]{:S(2)}, u32[]{:S(2)}) collective-permute-start(f32[1,4,4,4,128]{4,2,1,0,3:T(4,128)S(1)} %get-tuple-element.89), channel_id=1, source_target_pairs={{8,0},{16,8},{24,16},{9,1},{17,9},{25,17},{10,2},{18,10},{26,18},{... | collective-permute-start | bytes 98312 | tf_op jit(solution)/shard_map/ppermute | solution.py:317
  5.5 2.2 %collective-permute-start = (f32[1,4,4,4,128]{4,2,1,0,3:T(4,128)S(1)}, f32[1,4,4,4,128]{4,2,1,0,3:T(4,128)S(1)}, u32[]{:S(2)}, u32[]{:S(2)}) collective-permute-start(f32[1,4,4,4,128]{4,2,1,0,3:T(4,128)S(1)} %get-tuple-element.88), channel_id=1, source_target_pairs={{0,8},{8,16},{16,24},{1,9},{9,17},{17,25},{2,10},{10,18},{18,26},{... | collective-permute-start | bytes 98312 | tf_op jit(solution)/shard_map/ppermute | solution.py:316
  7.7 0.8 fusion.4
  8.5 0.9 copy-done.1
  9.4 1.6 shard_map.725
  11.1 4.0 %collective-permute-start.7 = (f32[3,4,4,128]{3,2,1,0:T(4,128)S(1)}, f32[3,4,4,128]{3,2,1,0:T(4,128)S(1)}, u32[]{:S(2)}, u32[]{:S(2)}) collective-permute-start(f32[3,4,4,128]{3,2,1,0:T(4,128)S(1)} %bitcast.86), channel_id=1, source_target_pairs={{8,0},{16,8},{24,16},{9,1},{17,9},{25,17},{10,2},{18,10},{26,18},{... | collective-permute-start | bytes 73736 | tf_op jit(solution)/shard_map/ppermute | solution.py:317
  15.0 1.9 collective-permute-start.6
  17.0 1.4 fusion.21
  18.4 0.4 fusion.22
  18.8 1.6 collective-permute-start.12
  20.6 0.6 collective-permute-done.12
  21.2 1.3 collective-permute-start.13
  22.5 3.1 %collective-permute-done.13 = f32[2,9,128]{2,1,0:T(8,128)S(1)} collective-permute-done((f32[2,9,128]{2,1,0:T(8,128)S(1)}, f32[2,9,128]{2,1,0:T(8,128)S(1)}, u32[]{:S(2)}, u32[]{:S(2)}) %collective-permute-start.13) | collective-permute-done | bytes 9248 | tf_op jit(solution)/shard_map/ppermute | solution.py:328
  25.7 0.5 collective-permute-start.14
  26.1 3.0 %collective-permute-done.14 = f32[2,9,128]{2,1,0:T(8,128)S(1)} collective-permute-done((f32[2,9,128]{2,1,0:T(8,128)S(1)}, f32[2,9,128]{2,1,0:T(8,128)S(1)}, u32[]{:S(2)}, u32[]{:S(2)}) %collective-permute-start.14) | collective-permute-done | bytes 9248 | tf_op jit(solution)/shard_map/ppermute | solution.py:328
  29.2 1.5 collective-permute-start.15
  30.7 1.1 collective-permute-done.15
  31.8 3.0 %collective-permute-start.17 = (f32[4,2,9,128]{3,2,1,0:T(8,128)S(1)}, f32[4,2,9,128]{3,2,1,0:T(8,128)S(1)}, u32[]{:S(2)}, u32[]{:S(2)}) collective-permute-start(f32[4,2,9,128]{3,2,1,0:T(8,128)S(1)} %bitcast_dynamic-update-slice_fusion.4), channel_id=1, source_target_pairs={{0,16},{8,24},{16,0},{24,8},{1,17},{9,25},{17,1},{25,9},{2,18},{10... | collective-permute-start | bytes 110600 | tf_op jit(solution)/shard_map/ppermute | solution.py:328
  34.9 0.7 fusion.18
  35.5 1.3 collective-permute-start.9
  36.8 4.0 %collective-permute-start.8 = (f32[10,3,4,128]{3,2,1,0:T(4,128)}, f32[10,3,4,128]{3,2,1,0:T(4,128)S(1)}, u32[]{:S(2)}, u32[]{:S(2)}) collective-permute-start(f32[10,3,4,128]{3,2,1,0:T(4,128)} %get-tuple-element.93), channel_id=1, source_target_pairs={{0,2},{2,4},{4,6},{1,3},{3,5},{5,7},{8,10},{10,12},{12,14},{9,11},... | collective-permute-start | bytes 184328 | tf_op jit(solution)/shard_map/ppermute | solution.py:316
  40.8 0.7 pad_maximum_fusion.13
  41.5 1.3 collective-permute-start.3
  42.8 4.0 %collective-permute-start.2 = (f32[6,1,4,4,128]{4,2,1,0,3:T(4,128)}, f32[6,1,4,4,128]{4,2,1,0,3:T(4,128)S(1)}, u32[]{:S(2)}, u32[]{:S(2)}) collective-permute-start(f32[6,1,4,4,128]{4,2,1,0,3:T(4,128)} %get-tuple-element.86), channel_id=1, source_target_pairs={{0,2},{2,4},{4,6},{1,3},{3,5},{5,7},{8,10},{10,12},{12,14},{9,11},... | collective-permute-start | bytes 147464 | tf_op jit(solution)/shard_map/ppermute | solution.py:316
  46.9 0.6 slice.439
  48.1 0.2 fusion.15
  49.2 1.6 slice_multiply_fusion.5
  51.2 0.8 copy.161
  52.9 0.8 copy.179
  53.7 0.8 copy.180
  54.5 0.8 copy.181
  55.4 0.8 copy.183
  56.2 0.8 copy.184
  57.0 0.8 copy.185
  58.6 1.9 multiply_reduce_fusion
  60.5 0.5 fusion.10
  61.3 7.3 %collective-permute-start.5 = (f32[6,6,1,4,128]{4,2,1,0,3:T(1,128)S(1)}, f32[6,6,1,4,128]{4,2,1,0,3:T(1,128)S(1)}, u32[]{:S(2)}, u32[]{:S(2)}) collective-permute-start(f32[6,6,1,4,128]{4,2,1,0,3:T(1,128)S(1)} %get-tuple-element.81), channel_id=1, source_target_pairs={{1,0},{3,2},{5,4},{7,6},{9,8},{11,10},{13,12},{15,14},{17,16},{19,... | collective-permute-start | bytes 221192 | tf_op jit(solution)/shard_map/ppermute | solution.py:317
  68.7 1.3 collective-permute-start.4
  70.2 3.0 %collective-permute-start.11 = (f32[10,10,3,128]{3,2,1,0:T(4,128)S(1)}, f32[10,10,3,128]{3,2,1,0:T(4,128)S(1)}, u32[]{:S(2)}, u32[]{:S(2)}) collective-permute-start(f32[10,10,3,128]{3,2,1,0:T(4,128)S(1)} %get-tuple-element.84), channel_id=1, source_target_pairs={{1,0},{3,2},{5,4},{7,6},{9,8},{11,10},{13,12},{15,14},{17,16},{19,... | collective-permute-start | bytes 460808 | tf_op jit(solution)/shard_map/ppermute | solution.py:317
  73.2 1.5 collective-permute-start.10
  74.7 0.2 pad_maximum_fusion
  74.9 0.3 copy.192
  75.3 71.9 %shard_map.724.near_ref = f32[64,128]{1,0:T(8,128)S(1)} custom-call(s32[64]{0:T(128)S(1)} %lt.74.counts_ref, f32[216,8,128]{2,1,0:T(8,128)S(1)} %bitcast.64), custom_call_target="tpu_custom_call" | custom-call | tf_op jit(solution)/shard_map/pallas_call | solution.py:249
  148.2 1.7 slice_multiply_fusion
  149.9 2.1 stack.183
  152.0 1.9 constant_dynamic-update-slice_fusion.6
  153.9 2.1 stack.184
  156.0 2.1 stack.185
  158.0 2.1 %stack.186 = f32[1,10,16,896]{3,2,1,0:T(8,128)} reshape(f32[10,4,4,896]{3,2,1,0:T(4,128)} %get-tuple-element.12) | data formatting | bytes 1146880 | tf_op jit(solution)/shard_map/stack | solution.py:395
  160.1 1.0 stack.187
  161.2 0.2 stack.188
  161.4 0.2 stack.189
  161.6 2.0 constant_dynamic-update-slice_fusion.5
  163.6 0.9 constant_dynamic-update-slice_fusion.4
  164.5 0.8 constant_dynamic-update-slice_fusion.3
  165.3 0.8 constant_dynamic-update-slice_fusion.2
  166.2 0.8 constant_dynamic-update-slice_fusion.1
  167.0 0.9 constant_dynamic-update-slice_fusion.leaf_ref
  167.9 2.1 %copy-done = f32[7,10,16,896]{3,2,1,0:T(8,128)S(1)} copy-done((f32[7,10,16,896]{3,2,1,0:T(8,128)S(1)}, f32[7,10,16,896]{3,2,1,0:T(8,128)}, u32[]{:S(2)}) %copy-start) | copy-done | bytes 4014104
  170.0 32.7 %shard_map.726 = f32[72,128]{1,0:T(8,128)S(1)} custom-call(f32[7,10,16,896]{3,2,1,0:T(8,128)S(1)} %copy-done, f32[49,8,896]{2,1,0:T(8,128)S(1)} %constant_dynamic-update-slice_fusion.14.mid_ref, bf16[49,896,256]{2,1,0:T(8,128)(2,1)} %constant.128.clone.table_ref), custom_call_target="tpu_custom_call" | custom-call | tf_op jit(solution)/shard_map/pallas_call | solution.py:296
  202.7 0.4 fusion.7
  203.1 4.2 %shard_map.727 = (f32[64,128]{1,0:T(8,128)}, f32[64,128]{1,0:T(8,128)}, f32[64,128]{1,0:T(8,128)}) custom-call(f32[3,64,128]{2,1,0:T(8,128)S(1)} %bitcast.70, f32[64,128]{1,0:T(8,128)S(1)} %bitcast.72, f32[64,128]{1,0:T(8,128)S(1)} %fusion.5.live_ref, f32[64,128]{1,0:T(8,128)S(1)} %shard_map.724.near_ref, f32[64,128]{1,0:T(8,128)S(1)} %get-tuple-element.96.total_ref, ...), custom_call_target="tpu_custom_call" | custom-call | tf_op jit(solution)/shard_map/pallas_call | solution.py:199
  (250 shorter events, 4.6 us)
Async XLA Ops:
  0.6 17.8 %copy-start.6 = (f32[1024,128]{1,0:T(8,128)S(1)}, f32[1024,128]{1,0:T(8,128)}, u32[]{:S(2)}) copy-start(f32[1024,128]{1,0:T(8,128)} %constant.112.clone) | copy-start | bytes 1572868
  0.6 19.8 %copy-start.13 = (s32[4,4,4]{2,1,0:T(4,128)S(1)}, s32[4,4,4]{2,1,0:T(4,128)}, u32[]{:S(2)}) copy-start(s32[4,4,4]{2,1,0:T(4,128)} %param.79) | copy-start | bytes 772
  2.4 33.2 %collective-permute-start.1 = (f32[1,4,4,4,128]{4,2,1,0,3:T(4,128)S(1)}, f32[1,4,4,4,128]{4,2,1,0,3:T(4,128)S(1)}, u32[]{:S(2)}, u32[]{:S(2)}) collective-permute-start(f32[1,4,4,4,128]{4,2,1,0,3:T(4,128)S(1)} %get-tuple-element.89), channel_id=1, source_target_pairs={{8,0},{16,8},{24,16},{9,1},{17,9},{25,17},{10,2},{18,10},{26,18},{... | collective-permute-start | bytes 98312 | tf_op jit(solution)/shard_map/ppermute | solution.py:317
  5.5 31.4 %collective-permute-start = (f32[1,4,4,4,128]{4,2,1,0,3:T(4,128)S(1)}, f32[1,4,4,4,128]{4,2,1,0,3:T(4,128)S(1)}, u32[]{:S(2)}, u32[]{:S(2)}) collective-permute-start(f32[1,4,4,4,128]{4,2,1,0,3:T(4,128)S(1)} %get-tuple-element.88), channel_id=1, source_target_pairs={{0,8},{8,16},{16,24},{1,9},{9,17},{17,25},{2,10},{10,18},{18,26},{... | collective-permute-start | bytes 98312 | tf_op jit(solution)/shard_map/ppermute | solution.py:316
  8.5 0.9 copy-start.1
  11.1 20.7 %collective-permute-start.7 = (f32[3,4,4,128]{3,2,1,0:T(4,128)S(1)}, f32[3,4,4,128]{3,2,1,0:T(4,128)S(1)}, u32[]{:S(2)}, u32[]{:S(2)}) collective-permute-start(f32[3,4,4,128]{3,2,1,0:T(4,128)S(1)} %bitcast.86), channel_id=1, source_target_pairs={{8,0},{16,8},{24,16},{9,1},{17,9},{25,17},{10,2},{18,10},{26,18},{... | collective-permute-start | bytes 73736 | tf_op jit(solution)/shard_map/ppermute | solution.py:317
  15.0 19.8 %collective-permute-start.6 = (f32[3,4,4,128]{3,2,1,0:T(4,128)S(1)}, f32[3,4,4,128]{3,2,1,0:T(4,128)S(1)}, u32[]{:S(2)}, u32[]{:S(2)}) collective-permute-start(f32[3,4,4,128]{3,2,1,0:T(4,128)S(1)} %bitcast.85), channel_id=1, source_target_pairs={{0,8},{8,16},{16,24},{1,9},{9,17},{17,25},{2,10},{10,18},{18,26},{... | collective-permute-start | bytes 73736 | tf_op jit(solution)/shard_map/ppermute | solution.py:316
  18.8 2.4 %collective-permute-start.12 = (f32[9,128]{1,0:T(8,128)S(1)}, f32[9,128]{1,0:T(8,128)S(1)}, u32[]{:S(2)}, u32[]{:S(2)}) collective-permute-start(f32[9,128]{1,0:T(8,128)S(1)} %pad_maximum_fusion.18), channel_id=1, source_target_pairs={{0,1},{1,0},{2,3},{3,2},{4,5},{5,4},{6,7},{7,6},{8,9},{9,8},{10,11... | collective-permute-start | bytes 13832 | tf_op jit(solution)/shard_map/ppermute | solution.py:328
  21.2 4.4 %collective-permute-start.13 = (f32[2,9,128]{2,1,0:T(8,128)S(1)}, f32[2,9,128]{2,1,0:T(8,128)S(1)}, u32[]{:S(2)}, u32[]{:S(2)}) collective-permute-start(f32[2,9,128]{2,1,0:T(8,128)S(1)} %bitcast_dynamic-update-slice_fusion.8), channel_id=1, source_target_pairs={{0,2},{2,4},{4,6},{6,0},{1,3},{3,5},{5,7},{7,1},{8,10},{10,12},{12... | collective-permute-start | bytes 27656 | tf_op jit(solution)/shard_map/ppermute | solution.py:328
  25.7 3.5 %collective-permute-start.14 = (f32[2,9,128]{2,1,0:T(8,128)S(1)}, f32[2,9,128]{2,1,0:T(8,128)S(1)}, u32[]{:S(2)}, u32[]{:S(2)}) collective-permute-start(f32[2,9,128]{2,1,0:T(8,128)S(1)} %bitcast_dynamic-update-slice_fusion.8), channel_id=1, source_target_pairs={{0,4},{2,6},{4,0},{6,2},{1,5},{3,7},{5,1},{7,3},{8,12},{10,14},{12... | collective-permute-start | bytes 27656 | tf_op jit(solution)/shard_map/ppermute | solution.py:328
  29.2 2.6 %collective-permute-start.15 = (f32[2,9,128]{2,1,0:T(8,128)S(1)}, f32[2,9,128]{2,1,0:T(8,128)S(1)}, u32[]{:S(2)}, u32[]{:S(2)}) collective-permute-start(f32[2,9,128]{2,1,0:T(8,128)S(1)} %bitcast_dynamic-update-slice_fusion.8), channel_id=1, source_target_pairs={{0,6},{2,0},{4,2},{6,4},{1,7},{3,1},{5,3},{7,5},{8,14},{10,8},{12,... | collective-permute-start | bytes 27656 | tf_op jit(solution)/shard_map/ppermute | solution.py:328
  31.8 9.8 %collective-permute-start.16 = (f32[4,2,9,128]{3,2,1,0:T(8,128)S(1)}, f32[4,2,9,128]{3,2,1,0:T(8,128)S(1)}, u32[]{:S(2)}, u32[]{:S(2)}) collective-permute-start(f32[4,2,9,128]{3,2,1,0:T(8,128)S(1)} %bitcast_dynamic-update-slice_fusion.4), channel_id=1, source_target_pairs={{0,8},{8,16},{16,24},{24,0},{1,9},{9,17},{17,25},{25,1},{2,10},{10... | collective-permute-start | bytes 110600 | tf_op jit(solution)/shard_map/ppermute | solution.py:328
  31.8 11.0 %collective-permute-start.17 = (f32[4,2,9,128]{3,2,1,0:T(8,128)S(1)}, f32[4,2,9,128]{3,2,1,0:T(8,128)S(1)}, u32[]{:S(2)}, u32[]{:S(2)}) collective-permute-start(f32[4,2,9,128]{3,2,1,0:T(8,128)S(1)} %bitcast_dynamic-update-slice_fusion.4), channel_id=1, source_target_pairs={{0,16},{8,24},{16,0},{24,8},{1,17},{9,25},{17,1},{25,9},{2,18},{10... | collective-permute-start | bytes 110600 | tf_op jit(solution)/shard_map/ppermute | solution.py:328
  34.8 12.1 %collective-permute-start.18 = (f32[4,2,9,128]{3,2,1,0:T(8,128)S(1)}, f32[4,2,9,128]{3,2,1,0:T(8,128)S(1)}, u32[]{:S(2)}, u32[]{:S(2)}) collective-permute-start(f32[4,2,9,128]{3,2,1,0:T(8,128)S(1)} %bitcast_dynamic-update-slice_fusion.4), channel_id=1, source_target_pairs={{0,24},{8,0},{16,8},{24,16},{1,25},{9,1},{17,9},{25,17},{2,26},{10... | collective-permute-start | bytes 110600 | tf_op jit(solution)/shard_map/ppermute | solution.py:328
  34.8 13.2 %copy-start.23 = (f32[2]{0:T(128)S(1)}, f32[2]{0:T(128)}, u32[]{:S(2)}) copy-start(f32[2]{0:T(128)} %constant.140) | copy-start | bytes 28
  34.8 13.3 %copy-start.20 = (f32[2,2]{1,0:T(2,128)S(1)}, f32[2,2]{1,0:T(2,128)}, u32[]{:S(2)}) copy-start(f32[2,2]{1,0:T(2,128)} %constant.143) | copy-start | bytes 52
  34.8 13.3 %copy-start.21 = (f32[2,2]{1,0:T(2,128)S(1)}, f32[2,2]{1,0:T(2,128)}, u32[]{:S(2)}) copy-start(f32[2,2]{1,0:T(2,128)} %constant.142) | copy-start | bytes 52
  34.9 13.3 %copy-start.22 = (f32[2,2]{1,0:T(2,128)S(1)}, f32[2,2]{1,0:T(2,128)}, u32[]{:S(2)}) copy-start(f32[2,2]{1,0:T(2,128)} %constant.141) | copy-start | bytes 52
  35.5 34.5 %collective-permute-start.9 = (f32[10,3,4,128]{3,2,1,0:T(4,128)}, f32[10,3,4,128]{3,2,1,0:T(4,128)S(1)}, u32[]{:S(2)}, u32[]{:S(2)}) collective-permute-start(f32[10,3,4,128]{3,2,1,0:T(4,128)} %get-tuple-element.94), channel_id=1, source_target_pairs={{2,0},{4,2},{6,4},{3,1},{5,3},{7,5},{10,8},{12,10},{14,12},{11,9},... | collective-permute-start | bytes 184328 | tf_op jit(solution)/shard_map/ppermute | solution.py:317
  36.8 33.2 %collective-permute-start.8 = (f32[10,3,4,128]{3,2,1,0:T(4,128)}, f32[10,3,4,128]{3,2,1,0:T(4,128)S(1)}, u32[]{:S(2)}, u32[]{:S(2)}) collective-permute-start(f32[10,3,4,128]{3,2,1,0:T(4,128)} %get-tuple-element.93), channel_id=1, source_target_pairs={{0,2},{2,4},{4,6},{1,3},{3,5},{5,7},{8,10},{10,12},{12,14},{9,11},... | collective-permute-start | bytes 184328 | tf_op jit(solution)/shard_map/ppermute | solution.py:316
  41.5 19.6 %collective-permute-start.3 = (f32[6,1,4,4,128]{4,2,1,0,3:T(4,128)}, f32[6,1,4,4,128]{4,2,1,0,3:T(4,128)S(1)}, u32[]{:S(2)}, u32[]{:S(2)}) collective-permute-start(f32[6,1,4,4,128]{4,2,1,0,3:T(4,128)} %get-tuple-element.87), channel_id=1, source_target_pairs={{2,0},{4,2},{6,4},{3,1},{5,3},{7,5},{10,8},{12,10},{14,12},{11,9},... | collective-permute-start | bytes 147464 | tf_op jit(solution)/shard_map/ppermute | solution.py:317
  42.8 18.3 %collective-permute-start.2 = (f32[6,1,4,4,128]{4,2,1,0,3:T(4,128)}, f32[6,1,4,4,128]{4,2,1,0,3:T(4,128)S(1)}, u32[]{:S(2)}, u32[]{:S(2)}) collective-permute-start(f32[6,1,4,4,128]{4,2,1,0,3:T(4,128)} %get-tuple-element.86), channel_id=1, source_target_pairs={{0,2},{2,4},{4,6},{1,3},{3,5},{5,7},{8,10},{10,12},{12,14},{9,11},... | collective-permute-start | bytes 147464 | tf_op jit(solution)/shard_map/ppermute | solution.py:316
  47.7 1.0 copy-start.19
  48.3 0.9 copy-start.17
  48.3 0.9 copy-start.18
  51.0 1.7 copy-start.12
  51.0 4.3 %copy-start.11 = (f32[2,2,2,896]{3,1,2,0:T(2,128)S(1)}, f32[2,2,2,896]{3,1,2,0:T(2,128)}, u32[]{:S(2)}) copy-start(f32[2,2,2,896]{3,1,2,0:T(2,128)} %get-tuple-element.42) | copy-start | bytes 86020
  52.0 5.8 %copy-start.10 = (f32[2,2,2,896]{3,1,2,0:T(2,128)S(1)}, f32[2,2,2,896]{3,1,2,0:T(2,128)}, u32[]{:S(2)}) copy-start(f32[2,2,2,896]{3,1,2,0:T(2,128)} %get-tuple-element.18) | copy-start | bytes 86020
  52.0 5.8 %copy-start.9 = (f32[2,2,2,896]{3,1,2,0:T(2,128)S(1)}, f32[2,2,2,896]{3,1,2,0:T(2,128)}, u32[]{:S(2)}) copy-start(f32[2,2,2,896]{3,1,2,0:T(2,128)} %get-tuple-element.17) | copy-start | bytes 86020
  57.9 0.7 copy-start.14
  58.4 2.1 %copy-start.7 = (f32[8,128,128]{2,1,0:T(8,128)S(1)}, f32[8,128,128]{2,1,0:T(8,128)}, u32[]{:S(2)}) copy-start(f32[8,128,128]{2,1,0:T(8,128)} %constant.150) | copy-start | bytes 1572868
  61.3 13.4 %collective-permute-start.5 = (f32[6,6,1,4,128]{4,2,1,0,3:T(1,128)S(1)}, f32[6,6,1,4,128]{4,2,1,0,3:T(1,128)S(1)}, u32[]{:S(2)}, u32[]{:S(2)}) collective-permute-start(f32[6,6,1,4,128]{4,2,1,0,3:T(1,128)S(1)} %get-tuple-element.81), channel_id=1, source_target_pairs={{1,0},{3,2},{5,4},{7,6},{9,8},{11,10},{13,12},{15,14},{17,16},{19,... | collective-permute-start | bytes 221192 | tf_op jit(solution)/shard_map/ppermute | solution.py:317
  68.7 6.0 %collective-permute-start.4 = (f32[6,6,1,4,128]{4,2,1,0,3:T(1,128)S(1)}, f32[6,6,1,4,128]{4,2,1,0,3:T(1,128)S(1)}, u32[]{:S(2)}, u32[]{:S(2)}) collective-permute-start(f32[6,6,1,4,128]{4,2,1,0,3:T(1,128)S(1)} %get-tuple-element.80), channel_id=1, source_target_pairs={{0,1},{2,3},{4,5},{6,7},{8,9},{10,11},{12,13},{14,15},{16,17},{18,... | collective-permute-start | bytes 221192 | tf_op jit(solution)/shard_map/ppermute | solution.py:316
  70.2 77.1 %collective-permute-start.11 = (f32[10,10,3,128]{3,2,1,0:T(4,128)S(1)}, f32[10,10,3,128]{3,2,1,0:T(4,128)S(1)}, u32[]{:S(2)}, u32[]{:S(2)}) collective-permute-start(f32[10,10,3,128]{3,2,1,0:T(4,128)S(1)} %get-tuple-element.84), channel_id=1, source_target_pairs={{1,0},{3,2},{5,4},{7,6},{9,8},{11,10},{13,12},{15,14},{17,16},{19,... | collective-permute-start | bytes 460808 | tf_op jit(solution)/shard_map/ppermute | solution.py:317
  73.2 74.0 %collective-permute-start.10 = (f32[10,10,3,128]{3,2,1,0:T(4,128)S(1)}, f32[10,10,3,128]{3,2,1,0:T(4,128)S(1)}, u32[]{:S(2)}, u32[]{:S(2)}) collective-permute-start(f32[10,10,3,128]{3,2,1,0:T(4,128)S(1)} %get-tuple-element.85), channel_id=1, source_target_pairs={{0,1},{2,3},{4,5},{6,7},{8,9},{10,11},{12,13},{14,15},{16,17},{18,... | collective-permute-start | bytes 460808 | tf_op jit(solution)/shard_map/ppermute | solution.py:316
  75.3 72.1 %copy-start.15 = (f32[4]{0:T(128)S(1)}, f32[4]{0:T(128)}, u32[]{:S(2)}) copy-start(f32[4]{0:T(128)} %constant.135) | copy-start | bytes 52
  147.4 0.7 copy-start.16
  161.6 2.0 copy-start.5
  161.6 2.9 %copy-start.4 = (f32[1,10,16,896]{3,2,1,0:T(8,128)S(1)}, f32[1,10,16,896]{3,2,1,0:T(8,128)}, u32[]{:S(2)}) copy-start(f32[1,10,16,896]{3,2,1,0:T(8,128)} %stack.186) | copy-start | bytes 1720324
  163.6 1.7 copy-start.3
  167.9 2.1 %copy-start = (f32[7,10,16,896]{3,2,1,0:T(8,128)S(1)}, f32[7,10,16,896]{3,2,1,0:T(8,128)}, u32[]{:S(2)}) copy-start(f32[7,10,16,896]{3,2,1,0:T(8,128)} %constant_dynamic-update-slice_fusion.leaf_ref) | copy-start | bytes 12042244
  170.0 32.7 %copy-start.8 = (f32[128,1024]{1,0:T(8,128)S(1)}, f32[128,1024]{1,0:T(8,128)}, u32[]{:S(2)}) copy-start(f32[128,1024]{1,0:T(8,128)} %constant.130.clone) | copy-start | bytes 1572868
  170.0 33.1 %copy-start.2 = (f32[3,4,4,4,128]{4,3,2,1,0:T(4,128)S(1)}, f32[3,4,4,4,128]{4,3,2,1,0:T(4,128)}, u32[]{:S(2)}) copy-start(f32[3,4,4,4,128]{4,3,2,1,0:T(4,128)} %param.77) | copy-start | bytes 294916
